TPU v7x, 256 devices: a whole 4x4x8 slice. The times are simulated.
256 devices in a mesh: complex: 2 (over core), row: 8 (over z), col: 16 (over y, x).
Axes of the slice: x: 4, y: 4, z: 8, core: 2. Of those that a mesh axis runs over, the one named last changes fastest.
Arguments:
- pair_act: bfloat16 [768, 384, 128], P(('complex', 'row'), 'col'), parts along dimension 0, may hold values from -64 to 64, as said below
- cotangent: bfloat16 [768, 384, 128], P(('complex', 'row'), 'col'), parts along dimension 0, may hold values from -6 to 6
- ln_gain: float32 [128], replicated, may hold values from 0.1 to 1.9
- ln_shift: float32 [128], replicated, may hold values from -3 to 3
- w_proj: bfloat16 [128, 512], replicated, may hold values from -0.5 to 0.5
- gate_bias: float32 [128], replicated, may hold values from -4 to 4
- w_bias: bfloat16 [128, 4], replicated, may hold values from -64 to 64
- w_out: bfloat16 [128, 128], replicated, may hold values from -0.5 to 0.5
- residue_mask: int32 [768], P(('complex', 'col')), parts along dimension 0, may hold values 0 or 1
- valid_length: int32 [2], P('complex'), parts along dimension 0, may hold values from 96 to 384
Outputs:
- update: bfloat16 [768, 384, 128], P(('complex', 'row'), 'col'), parts along dimension 0
- pair_grad: bfloat16 [768, 384, 128], P(('complex', 'row'), 'col'), parts along dimension 0
- proj_grad: float32 [256, 512], P('complex'), parts along dimension 0
There are 2 independent parts, one for each index of `complex`. A program takes and returns all parts, laid end to end along the dimension named above; an argument that names none is the same for every part. Nothing has to cross between parts.
Inputs may be any that keep to these rules, and one draw needn't show every extreme that they name: `pair_act`: finite values.
All inputs are finite; a program needn't handle non-finite values. No bound on the sum of `residue_mask` on one device may be relied on, other than what follows from the above.
Results may differ from a plain program's by a relative error of at most 0.012.
The roundings to bfloat16 on the way count: a program that leaves them out, or rounds other values in their place, can miss the bound.
Values may be sent and summed in bfloat16 or wider, within the bound.
A program may use at most 128 MiB of HBM per device.

v0:
```python
import math

import jax
import jax.numpy as jnp
from jax import lax
from jax.sharding import PartitionSpec as P

neg_large = -1000000000.0
ln_eps = 1e-05


def spread(value, axis, root):
    mine = lax.axis_index(axis) == root
    return lax.psum(jnp.where(mine, value, jnp.zeros_like(value)), axis)


def normalize(activity, ln_gain, ln_shift):
    values = activity.astype(jnp.float32)
    centre = values - jnp.mean(values, axis=-1, keepdims=True)
    inverse = lax.rsqrt(jnp.mean(centre * centre, axis=-1, keepdims=True) + ln_eps)
    standard = centre * inverse
    normed = (standard * ln_gain + ln_shift).astype(jnp.bfloat16)
    return (normed, standard, inverse)


def project(normed, w_proj, gate_bias, w_bias):
    inner_width = w_proj.shape[1] // 4
    head_count = w_bias.shape[1]
    query_scale = (inner_width // head_count) ** (-0.5)
    flat_rows = normed.reshape(-1, normed.shape[-1])
    projected = jnp.dot(flat_rows, w_proj, preferred_element_type=jnp.float32)
    queries = (projected[:, :inner_width] * query_scale).astype(jnp.bfloat16)
    key_values = projected[:, inner_width : 3 * inner_width].astype(jnp.bfloat16)
    gate_value = jax.nn.sigmoid(projected[:, 3 * inner_width :] + gate_bias)
    logits = jnp.dot(flat_rows, w_bias, preferred_element_type=jnp.float32)
    return (queries, key_values, gate_value, logits)


def attend(queries, key_rows, value_rows, pair_bias, negative, d_attn, head_count):
    batch_rows, col_count, inner_width = queries.shape
    key_count = key_rows.shape[1]
    head_size = inner_width // head_count
    q_four = queries.reshape(batch_rows, col_count, head_count, head_size)
    k_four = key_rows.reshape(batch_rows, key_count, head_count, head_size)
    v_four = value_rows.reshape(batch_rows, key_count, head_count, head_size)
    d_four = d_attn.reshape(batch_rows, col_count, head_count, head_size)
    scores = (
        jnp.einsum("bjhd,bkhd->bhjk", q_four, k_four, preferred_element_type=jnp.float32)
        + pair_bias
        + negative
    )
    row_max = jnp.max(scores, axis=-1, keepdims=True)
    exponent = jnp.exp(scores - row_max)
    weights = exponent / jnp.sum(exponent, axis=-1, keepdims=True)
    weights_b = weights.astype(jnp.bfloat16)
    attended = jnp.einsum("bhjk,bkhd->bjhd", weights_b, v_four, preferred_element_type=jnp.float32)
    d_prob = jnp.einsum("bjhd,bkhd->bhjk", d_four, v_four, preferred_element_type=jnp.float32)
    d_score = weights * (d_prob - jnp.sum(weights * d_prob, axis=-1, keepdims=True))
    d_score_b = d_score.astype(jnp.bfloat16)
    d_values = jnp.einsum("bhjk,bjhd->bkhd", weights_b, d_four, preferred_element_type=jnp.float32)
    d_query = jnp.einsum("bhjk,bkhd->bjhd", d_score_b, k_four, preferred_element_type=jnp.float32)
    d_keys = jnp.einsum("bhjk,bjhd->bkhd", d_score_b, q_four, preferred_element_type=jnp.float32)
    d_keyval = jnp.concatenate(
        [
            d_keys.reshape(batch_rows, key_count, inner_width),
            d_values.reshape(batch_rows, key_count, inner_width),
        ],
        axis=-1,
    )
    return (
        attended.reshape(batch_rows, col_count, inner_width),
        d_query.reshape(batch_rows, col_count, inner_width),
        d_keyval,
        jnp.sum(d_score, axis=0),
    )


def attend_blocks(queries, key_values, pair_bias, negative, d_attn, head_count, block_rows):
    row_count, col_count, inner_width = queries.shape
    key_count = key_values.shape[1]
    block_count = row_count // block_rows

    def row_step(bias_total, block_index):
        row_start = block_index * block_rows
        q_part = lax.dynamic_slice_in_dim(queries, row_start, block_rows, 0)
        kv_part = lax.dynamic_slice_in_dim(key_values, row_start, block_rows, 0)
        d_part = lax.dynamic_slice_in_dim(d_attn, row_start, block_rows, 0)
        result = attend(
            q_part,
            kv_part[..., :inner_width],
            kv_part[..., inner_width:],
            pair_bias,
            negative,
            d_part,
            head_count,
        )
        return (bias_total + result[3], (result[0], result[1], result[2]))

    d_bias, (attended, d_query, d_keyval) = lax.scan(
        row_step,
        jnp.zeros((head_count, col_count, key_count), jnp.float32),
        jnp.arange(block_count),
    )
    return (
        attended.reshape(row_count, col_count, inner_width),
        d_query.reshape(row_count, col_count, inner_width),
        d_keyval.reshape(row_count, key_count, 2 * inner_width),
        d_bias,
    )


def attention_pass(
    queries,
    key_values,
    gate_value,
    pair_bias,
    all_flags,
    row_flags,
    query_flags,
    cotangent,
    w_out,
    block_rows,
    head_count,
):
    row_count = row_flags.shape[0]
    col_count = query_flags.shape[0]
    inner_width = w_out.shape[0]
    query_scale = (inner_width // head_count) ** (-0.5)
    pair_mask = (row_flags[:, None] * query_flags[None, :]).astype(jnp.float32).reshape(-1, 1)
    flat_cot = cotangent.reshape(-1, cotangent.shape[-1])
    d_out = jnp.where(pair_mask > 0, flat_cot, jnp.zeros((), jnp.bfloat16))
    d_gated = jnp.einsum("mc,hc->mh", d_out, w_out, preferred_element_type=jnp.float32)
    d_attn = (d_gated * gate_value).astype(jnp.bfloat16)
    negative = jnp.where(all_flags > 0, 0.0, neg_large).astype(jnp.float32)
    attended, d_query, d_keyval, d_bias = attend_blocks(
        queries.reshape(row_count, col_count, inner_width),
        key_values,
        pair_bias,
        negative,
        d_attn.reshape(row_count, col_count, inner_width),
        head_count,
        block_rows,
    )
    attended = attended.reshape(-1, inner_width)
    gated_out = (gate_value * attended).astype(jnp.bfloat16)
    update = (jnp.dot(gated_out, w_out, preferred_element_type=jnp.float32) * pair_mask).astype(
        jnp.bfloat16
    )
    d_gate_in = d_gated * attended * gate_value * (1.0 - gate_value)
    return (
        update.reshape(row_count, col_count, -1),
        d_query.reshape(-1, inner_width) * query_scale,
        d_keyval,
        d_gate_in,
        d_bias,
    )


def finish(d_proj, normed, standard, inverse, bias_grad, w_proj, w_bias, ln_gain):
    flat_rows = normed.reshape(-1, normed.shape[-1])
    bias_term = jnp.dot(bias_grad, w_bias.astype(jnp.float32).T, precision=lax.Precision.HIGHEST)
    d_normed = (
        jnp.einsum("mn,cn->mc", d_proj, w_proj, preferred_element_type=jnp.float32) + bias_term
    )
    weight_part = jnp.einsum("mc,mn->cn", flat_rows, d_proj, preferred_element_type=jnp.float32)
    weight_grad = lax.psum(weight_part, ("row", "col"))
    d_unit = d_normed.reshape(standard.shape) * ln_gain
    mean_grad = jnp.mean(d_unit, axis=-1, keepdims=True)
    mean_cross = jnp.mean(d_unit * standard, axis=-1, keepdims=True)
    pair_grad = (inverse * (d_unit - mean_grad - standard * mean_cross)).astype(jnp.bfloat16)
    return (pair_grad, weight_grad)


def valid_flags(residue_mask, valid_length):
    width_here = residue_mask.shape[0]
    positions = lax.axis_index("col") * width_here + lax.iota(jnp.int32, width_here)
    return jnp.where(positions < valid_length[0], residue_mask, 0)


def shards(
    pair_act,
    cotangent,
    ln_gain,
    ln_shift,
    w_proj,
    gate_bias,
    w_bias,
    w_out,
    residue_mask,
    valid_length,
):
    head_count = w_bias.shape[1]
    inner_width = w_out.shape[0]
    local_flags = valid_flags(residue_mask, valid_length)
    row_count, col_count, channels = pair_act.shape
    normed, standard, inverse = normalize(pair_act, ln_gain, ln_shift)
    queries, key_values, gate_value, logits = project(normed, w_proj, gate_bias, w_bias)
    key_values = key_values.reshape(row_count, col_count, 2 * inner_width)
    band_values, all_flags = (
        lax.all_gather(key_values, "col", axis=1, tiled=True),
        lax.all_gather(local_flags.astype(jnp.bfloat16), "col", axis=0, tiled=True),
    )
    row_flags = lax.dynamic_slice_in_dim(all_flags, lax.axis_index("row") * row_count, row_count)
    bias_piece = jnp.transpose(logits.reshape(row_count, col_count, head_count), (2, 0, 1))
    bias_band = lax.all_gather(bias_piece, "col", axis=2, tiled=True)
    owner_row = lax.axis_index("col") * col_count // row_count
    bias_band = spread(bias_band, "row", owner_row)
    pair_bias = lax.dynamic_slice_in_dim(
        bias_band, lax.axis_index("col") * col_count - owner_row * row_count, col_count, 1
    )
    update, d_query, d_keyval_part, d_gate_in, d_bias = attention_pass(
        queries,
        band_values,
        gate_value,
        pair_bias,
        all_flags,
        row_flags,
        local_flags,
        cotangent,
        w_out,
        math.gcd(row_count, 8),
        head_count,
    )
    d_keyval = lax.psum_scatter(d_keyval_part, "col", scatter_dimension=1, tiled=True)
    bias_sum = lax.psum(d_bias, "row")
    bias_cols = lax.all_to_all(bias_sum, "col", split_axis=2, concat_axis=1, tiled=True)
    bias_grad = lax.dynamic_slice_in_dim(bias_cols, lax.axis_index("row") * row_count, row_count, 1)
    d_proj = jnp.concatenate(
        [d_query, d_keyval.reshape(-1, 2 * inner_width), d_gate_in], axis=1
    ).astype(jnp.bfloat16)
    pair_grad, weight_grad = finish(
        d_proj,
        normed,
        standard,
        inverse,
        jnp.transpose(bias_grad, (1, 2, 0)).reshape(-1, head_count),
        w_proj,
        w_bias,
        ln_gain,
    )
    return (update, pair_grad, weight_grad)


def solution(mesh):
    return jax.shard_map(
        shards,
        mesh=mesh,
        in_specs=(
            P(("complex", "row"), "col", None),
            P(("complex", "row"), "col", None),
            P(),
            P(),
            P(),
            P(),
            P(),
            P(),
            P(("complex", "col")),
            P("complex"),
        ),
        out_specs=(
            P(("complex", "row"), "col", None),
            P(("complex", "row"), "col", None),
            P("complex", None),
        ),
        check_vma=False,
    )
```

profile of v0, /device:TPU:1, one launch (start us, length us, event | category | flops | bytes accessed | tf_op | source)
XLA Modules:
  0.0 620.2 jit_solution(17813282303872741747)
XLA Ops:
  12.8 20.3 %all_gather.10 = f32[4,48,384]{1,0,2:T(4,128)S(1)} all-gather(f32[4,48,24]{1,0,2:T(4,128)S(1)} %copy.33), channel_id=1, replica_groups=mesh['complex'=2,'row'=8,'col'=16] {'col'}, dimensions={2}, use_global_device_ids=true | all-gather | bytes 313344 | tf_op jit(solution)/shard_map/all_gather | solution.py:205
  38.1 31.1 %all-reduce = bf16[384]{0:T(512)(128)(2,1)S(1)} all-reduce(bf16[384]{0:T(512)(128)(2,1)S(1)} %dynamic-update-slice), channel_id=1, replica_groups=mesh['complex'=2,'row'=8,'col'=16] {'col'}, use_global_device_ids=true, to_apply=%add | all-reduce | flops 384 | bytes 1536
  71.0 40.9 %all-reduce.5.cloned.1.call-done = f32[4,48,384]{1,0,2:T(4,128)} async-done(((f32[4,48,384]{1,0,2:T(4,128)}), f32[4,48,384]{1,0,2:T(4,128)}) %all-reduce.5.cloned.1.call-update) | async-done | bytes 294928 | tf_op jit(solution)/shard_map/psum | solution.py:14
  114.5 9.2 %all-gather.2.cloned.1.call-done = bf16[48,384,256]{2,0,1:T(8,128)(2,1)} async-done(((bf16[48,24,256]{2,0,1:T(8,128)(2,1)}), bf16[48,384,256]{2,0,1:T(8,128)(2,1)}) %all-gather.2.cloned.1.call-update) | async-done | bytes 9437200 | tf_op jit(solution)/shard_map/all_gather | solution.py:200
  124.1 139.7 %while.17 = (s32[]{:T(128)}, f32[4,24,384]{2,1,0:T(8,128)}, f32[6,8,24,128]{3,2,1,0:T(8,128)}, f32[6,8,24,128]{3,2,1,0:T(8,128)}, f32[6,8,384,256]{3,2,1,0:T(8,1...) while((s32[]{:T(128)}, f32[4,24,384]{2,1,0:T(8,128)}, ...), condition=%wide.region_8.9_spmd.clone, body=%wide.region_3.8_spmd.clone.sunk | while | flops 118787720 | bytes 48536492 | solution.py:99
  142.2 2.4 copy.82
  144.6 2.0 constant_dynamic-update-slice_fusion.6
  165.7 2.4 copy.82
  168.1 2.0 constant_dynamic-update-slice_fusion.6
  189.2 2.4 copy.82
  191.6 2.0 constant_dynamic-update-slice_fusion.6
  212.7 2.4 copy.82
  215.0 2.0 constant_dynamic-update-slice_fusion.6
  236.1 2.4 copy.82
  238.5 2.0 constant_dynamic-update-slice_fusion.6
  259.5 2.4 copy.82
  261.9 2.0 constant_dynamic-update-slice_fusion.6
  263.9 2.1 copy.37
  269.1 67.9 %all-reduce.7.cloned.1.call-done = f32[4,24,384]{1,0,2:T(4,128)} async-done(((f32[4,24,384]{1,0,2:T(4,128)}), f32[4,24,384]{1,0,2:T(4,128)}) %all-reduce.7.cloned.1.call-update) | async-done | bytes 147472 | tf_op jit(solution)/shard_map/psum | solution.py:225
  337.1 2.8 reshape.157
  339.9 6.3 %all-to-all-start = ((f32[16,1,2304]{2,1,0:T(1,128)}), f32[16,1,2304]{2,1,0:T(1,128)S(1)}, u32[]{:S(2)}, u32[]{:S(2)}) async-start(f32[16,1,2304]{2,1,0:T(1,128)} %reshape.157), calls=%async_computation.1 | async-start | bytes 294912 | tf_op jit(solution)/shard_map/all_to_all | solution.py:226
  347.4 7.5 %all-to-all-done = f32[16,1,2304]{2,1,0:T(1,128)S(1)} async-done(((f32[16,1,2304]{2,1,0:T(1,128)}), f32[16,1,2304]{2,1,0:T(1,128)S(1)}, u32[]{:S(2)}, u32[]{:S(2)}) %all-to-all-start) | async-done | bytes 147488 | tf_op jit(solution)/shard_map/all_to_all | solution.py:226
  358.6 39.5 %reduce-scatter.2.cloned.1.call-done = f32[48,24,256]{2,1,0:T(8,128)} async-done(((f32[48,384,256]{2,1,0:T(8,128)}), f32[48,24,256]{2,1,0:T(8,128)}) %reduce-scatter.2.cloned.1.call-update) | async-done | bytes 1179664 | tf_op jit(solution)/shard_map/reduce_scatter | solution.py:224
  404.5 207.0 %all-reduce.9.cloned.1.call-done = f32[128,512]{1,0:T(8,128)} async-done(((f32[128,512]{1,0:T(8,128)}), f32[128,512]{1,0:T(8,128)}) %all-reduce.9.cloned.1.call-update) | async-done | bytes 262160 | tf_op jit(solution)/shard_map/psum | solution.py:166
  (298 shorter events, 137.9 us)
Async XLA Ops:
  8.0 26.2 %copy-start = (bf16[128,512]{1,0:T(8,128)(2,1)S(1)}, bf16[128,512]{1,0:T(8,128)(2,1)}, u32[]{:S(2)}) copy-start(bf16[128,512]{1,0:T(8,128)(2,1)} %param.16) | copy-start | bytes 393220
  8.0 4.0 copy-start.18
  8.0 103.9 %all-reduce.5.cloned.1.call-start = ((), (), s32[]{:S(2)}) async-start(), calls=%async_computation.3 | async-start | bytes 1572864 | tf_op jit(solution)/shard_map/psum | solution.py:14
  12.1 22.2 %copy-start.9 = (bf16[48,24,128]{2,1,0:T(8,128)(2,1)}, bf16[48,24,128]{2,1,0:T(8,128)(2,1)S(1)}, u32[]{:S(2)}) copy-start(bf16[48,24,128]{2,1,0:T(8,128)(2,1)S(1)} %fusion.24) | copy-start | bytes 884740
  34.2 89.4 %all-gather.2.cloned.1.call-start = ((), (), s32[]{:S(2)}) async-start(), calls=%async_computation.2 | async-start | bytes 10027008 | tf_op jit(solution)/shard_map/all_gather | solution.py:200
  34.7 35.0 %copy-start.6 = (f32[1152,512]{1,0:T(8,128)}, f32[1152,512]{1,0:T(8,128)S(1)}, u32[]{:S(2)}) copy-start(f32[1152,512]{1,0:T(8,128)S(1)} %fusion.48) | copy-start | bytes 7077892
  34.8 1.8 copy-start.22
  34.8 3.0 copy-start.21
  34.8 34.7 %copy-start.14 = (bf16[48,24,128]{2,1,0:T(8,128)(2,1)S(1)}, bf16[48,24,128]{2,1,0:T(8,128)(2,1)}, u32[]{:S(2)}) copy-start(bf16[48,24,128]{2,1,0:T(8,128)(2,1)} %param.13) | copy-start | bytes 884740
  34.8 34.9 %copy-start.15 = (bf16[128,128]{1,0:T(8,128)(2,1)S(1)}, bf16[128,128]{1,0:T(8,128)(2,1)}, u32[]{:S(2)}) copy-start(bf16[128,128]{1,0:T(8,128)(2,1)} %param.19) | copy-start | bytes 98308
  34.8 34.9 %copy-start.19 = (f32[128]{0:T(128)S(1)}, f32[128]{0:T(128)}, u32[]{:S(2)}) copy-start(f32[128]{0:T(128)} %param.17) | copy-start | bytes 1540
  35.8 301.2 %all-reduce.7.cloned.1.call-start = ((), (), s32[]{:S(2)}) async-start(), calls=%async_computation.5 | async-start | bytes 1572864 | tf_op jit(solution)/shard_map/psum | solution.py:225
  129.0 2.9 copy-start.1
  151.5 3.0 copy-start.1
  155.4 1.6 copy-start.7
  175.0 3.0 copy-start.1
  198.5 3.0 copy-start.1
  221.9 3.0 copy-start.1
  245.3 2.9 copy-start.1
  249.2 1.6 copy-start.7
  266.0 132.0 %reduce-scatter.2.cloned.1.call-start = ((), (), s32[]{:S(2)}) async-start(), calls=%async_computation.4 | async-start | bytes 20054016 | tf_op jit(solution)/shard_map/reduce_scatter | solution.py:224
  269.1 77.3 %copy-start.16 = (bf16[128,128]{1,0:T(8,128)(2,1)S(1)}, bf16[128,128]{1,0:T(8,128)(2,1)}, u32[]{:S(2)}) copy-start(bf16[128,128]{1,0:T(8,128)(2,1)} %param.19) | copy-start | bytes 98308
  339.9 15.0 %all-to-all-start = ((f32[16,1,2304]{2,1,0:T(1,128)}), f32[16,1,2304]{2,1,0:T(1,128)S(1)}, u32[]{:S(2)}, u32[]{:S(2)}) async-start(f32[16,1,2304]{2,1,0:T(1,128)} %reshape.157), calls=%async_computation.1 | async-start | bytes 294912 | tf_op jit(solution)/shard_map/all_to_all | solution.py:226
  346.2 265.3 %all-reduce.9.cloned.1.call-start = ((), (), s32[]{:S(2)}) async-start(), calls=%async_computation.6 | async-start | bytes 524288 | tf_op jit(solution)/shard_map/psum | solution.py:166
  (35 other events, 43.2 us)
Sparse Core Ops, SparseCore 0:
  34.3 77.5 all-reduce.4
  266.1 70.9 all-reduce.6
  403.1 208.3 all-reduce.8
Sparse Core Ops, SparseCore 1:
  37.1 86.5 all-gather.1
  270.7 127.3 reduce-scatter.1
where the time goes:
time: 626 us; the launch traced here: 620 us
  waiting for transfers between devices  372 us (59%)
  local copies, waits for them, and re-layouts  99.6 us (16%)
  blocking collectives  51.4 us (8%)
  matrix products  35.3 us (6%)
  other arithmetic  33.2 us (5%)
  between operations  17 us (3%)
  starting transfers between devices  6.71 us (1%)
    psum x1, waiting for transfers between devices, finish(): weight_grad = lax.psum(weight_part, ('row', 'col'))  207 us
    psum x1, waiting for transfers between devices, shards(): bias_sum = lax.psum(d_bias, 'row')  67.9 us
    psum x1, waiting for transfers between devices, spread(): return lax.psum(jnp.where(mine, value, jnp.zeros_like(value)), axis)  40.9 us
    reduce_scatter x1, waiting for transfers between devices, shards(): lax.psum_scatter(d_keyval_part, 'col', scatter_dimension=1, tiled=True)  39.5 us
    unnamed x1, blocking collectives  31.1 us
    dynamic_update_slice x18, local copies, waits for them, and re-layouts, attend_blocks(): lax.scan(row_step, jnp.zeros((head_count, col_count, key_count), jnp.floa...  30.5 us
    all_gather x1, blocking collectives, shards(): bias_band = lax.all_gather(bias_piece, 'col', axis=2, tiled=True)  20.3 us
    while x84, local copies, waits for them, and re-layouts  17.6 us
  transfers between devices with their start and end apart: 6, of which 6 were waited for; matrix products, arithmetic and copies ran while one was open for 3% of the time, Pallas kernels for 0%

commit v1 on v0

v1 whole, which is shorter than its diff:
```python
import jax
import jax.numpy as jnp
from jax import lax
from jax.experimental import pallas as pl
from jax.experimental.pallas import tpu as pltpu
from jax.sharding import PartitionSpec as P

MESH = pl.DeviceIdType.MESH
F32 = jnp.float32
BF16 = jnp.bfloat16
N = 384
C = 128
H = 4
DH = 32
HD = H * DH
COLS = 16
WIDTH = N // COLS
OWN = 3
PART = OWN * WIDTH
INBOX = 176
VMEM_LIMIT = 60 * 1024 * 1024
NT = (((1,), (1,)), ((), ()))
TN = (((0,), (0,)), ((), ()))


class Place:
    def __init__(self):
        self.e = lax.axis_index("complex")
        self.z = lax.axis_index("row")
        self.c = lax.axis_index("col")
        self.part = lax.rem(self.z, 2)
        self.zz = lax.div(self.z, 2)
        self.y = lax.div(self.c, 4)
        self.x = lax.rem(self.c, 4)
        self.f, self.g = self.axes(self.e)
        self.swap_z = self.zz * 2 + self.e
        self.stays = self.part == self.e
        self.row0 = (self.zz * 2 + self.e) * (COLS * OWN) + self.c * OWN

    def axes(self, e):
        return self.x * (1 - e) + self.y * e, self.y * (1 - e) + self.x * e

    def col(self, e, f, g):
        return lax.rem(f, 4) * (1 + 3 * e) + lax.rem(g, 4) * (4 - 3 * e)

    def swapped(self, c):
        return (self.part, self.swap_z, c)

    def zpeer(self, d):
        return (self.e, lax.rem(self.zz + d, 4) * 2 + self.part, self.c)

    def fpeer(self, d):
        return (self.e, self.z, self.col(self.e, self.f + d, self.g))

    def gpeer(self, d):
        return (self.e, self.z, self.col(self.e, self.f, self.g + d))

    def partner(self):
        return (1 - self.e, self.z, self.c)


def remote(src, dst, send, recv, device):
    return pltpu.make_async_remote_copy(
        src_ref=src, dst_ref=dst, send_sem=send, recv_sem=recv, device_id=device, device_id_type=MESH
    )


def arrived(ref, sem):
    pltpu.make_async_copy(ref, ref, sem).wait()


def greet(device):
    pl.semaphore_signal(pltpu.get_barrier_semaphore(), inc=1, device_id=device, device_id_type=MESH)


def greet_common(at):
    def column(d, carry):
        @pl.when(jnp.logical_or(d > 0, jnp.logical_not(at.stays)))
        def _():
            greet(at.swapped(lax.rem(at.c + d, COLS)))

        return carry

    lax.fori_loop(0, COLS, column, 0)
    for d in (1, 2, 3):
        greet(at.zpeer(d))
        greet(at.fpeer(d))
        greet(at.gpeer(d))
    greet(at.partner())
    return COLS + 10 - at.stays.astype(jnp.int32)


def exchange_start(at, source, landing, send, recv):
    def column(d, carry):
        t = lax.rem(at.c + d, COLS)
        here = jnp.logical_and(d == 0, at.stays)

        @pl.when(here)
        def _():
            pltpu.make_async_copy(source.at[t], landing.at[at.c], recv.at[at.c]).start()

        @pl.when(jnp.logical_not(here))
        def _():
            remote(source.at[t], landing.at[at.c], send.at[t], recv.at[at.c], at.swapped(t)).start()

        return carry

    lax.fori_loop(0, COLS, column, 0)


def exchange_arrived(landing, recv):
    def column(d, carry):
        arrived(landing.at[d], recv.at[d])
        return carry

    lax.fori_loop(0, COLS, column, 0)


def exchange_sent(at, source, send):
    def column(d, carry):
        t = lax.rem(at.c + d, COLS)

        @pl.when(jnp.logical_or(d > 0, jnp.logical_not(at.stays)))
        def _():
            arrived(source.at[t], send.at[t])

        return carry

    lax.fori_loop(0, COLS, column, 0)


def gather_kernel(
    msg,
    gain,
    shift,
    w_proj,
    w_proj_t,
    gate_bias,
    w_bias_t,
    w_out,
    bias,
    normed,
    standard,
    rstd,
    q,
    k,
    v,
    d,
    q_t,
    k_t,
    v_t,
    d_t,
    gate,
    dgate,
    mask,
    inbox,
    in_send,
    in_recv,
    z_send,
    z_recv,
    f_send,
    f_recv,
    g_send,
    g_recv,
    p_send,
    p_recv,
):
    at = Place()
    count = greet_common(at)
    pl.semaphore_wait(pltpu.get_barrier_semaphore(), count)
    exchange_start(at, msg, inbox, in_send, in_recv)
    exchange_arrived(inbox, in_recv)
    mask[...] = inbox[:, 2 * PART : 2 * PART + WIDTH, :].astype(F32).reshape(N, C)


    for s in range(OWN):
        values = inbox[:, s * WIDTH : (s + 1) * WIDTH, :].astype(F32).reshape(N, C)
        centre = values - jnp.mean(values, axis=-1, keepdims=True)
        inverse = lax.rsqrt(jnp.mean(centre * centre, axis=-1, keepdims=True) + 1e-5)
        unit = centre * inverse
        standard[s] = unit
        rstd[s] = jnp.broadcast_to(inverse, (N, C))
        rows = (unit * gain[...] + shift[...]).astype(BF16)
        normed[s] = rows
        logits = lax.dot_general(w_bias_t[...], rows, NT, preferred_element_type=F32)
        bias[at.zz, at.e, at.c, s] = logits[:H]

    mine = bias.at[at.zz, at.e, at.c]
    for n in (1, 2, 3):
        remote(mine, mine, z_send.at[n - 1], z_recv.at[n - 1], at.zpeer(n)).start()

    def project(s):
        rows = normed[s]
        flat = jnp.dot(rows, w_proj[...], preferred_element_type=F32)
        q[s] = (flat[:, :HD] * DH ** (-0.5)).astype(BF16)
        k[s] = flat[:, HD : 2 * HD].astype(BF16)
        v[s] = flat[:, 2 * HD : 3 * HD].astype(BF16)
        gates = jax.nn.sigmoid(flat[:, 3 * HD :] + gate_bias[...])
        flat_t = lax.dot_general(w_proj_t[...], rows, NT, preferred_element_type=F32)
        q_t[s] = (flat_t[:HD] * DH ** (-0.5)).astype(BF16)
        k_t[s] = flat_t[HD : 2 * HD].astype(BF16)
        v_t[s] = flat_t[2 * HD : 3 * HD].astype(BF16)
        cot = inbox[:, PART + s * WIDTH : PART + (s + 1) * WIDTH, :].astype(F32).reshape(N, C)
        pair = mask[...] * mask[pl.ds(at.row0 + s, 1), :]
        d_out = jnp.where(pair > 0, cot, 0.0).astype(BF16)
        d_gated = lax.dot_general(d_out, w_out[...], NT, preferred_element_type=F32)
        d_attn = d_gated * gates
        d[s] = d_attn.astype(BF16)
        d_t[s] = d_attn.T.astype(BF16)
        gate[s] = gates
        dgate[s] = d_gated * gates * (1.0 - gates)

    def chunk(ref, e, c):
        return ref.at[:, e, c]

    def to_partner(a, b):
        part = chunk(bias, at.e, at.col(at.e, at.f - a + 4, at.g - b + 4))
        remote(part, part, p_send.at[a, b], p_recv.at[a, b], at.partner()).start()

    def to_second(a):
        part = chunk(bias, at.e, at.col(at.e, at.f - a + 4, at.g))
        for n in (1, 2, 3):
            remote(part, part, g_send.at[a, n - 1], g_recv.at[a, n - 1], at.gpeer(n)).start()

    project(0)
    for n in (1, 2, 3):
        arrived(bias.at[lax.rem(at.zz - n + 4, 4), at.e, at.c], z_recv.at[n - 1])
    own = chunk(bias, at.e, at.c)
    for n in (1, 2, 3):
        remote(own, own, f_send.at[n - 1], f_recv.at[n - 1], at.fpeer(n)).start()
    to_second(0)
    to_partner(0, 0)
    project(1)
    for n in (1, 2, 3):
        part = chunk(bias, at.e, at.col(at.e, at.f - n + 4, at.g))
        arrived(part, f_recv.at[n - 1])
        to_second(n)
        to_partner(n, 0)
    project(2)
    for a in range(4):
        for n in (1, 2, 3):
            part = chunk(bias, at.e, at.col(at.e, at.f - a + 4, at.g - n + 4))
            arrived(part, g_recv.at[a, n - 1])
            to_partner(a, n)
    other = 1 - at.e
    f_other, g_other = at.axes(other)
    for a in range(4):
        for b in range(4):
            part = chunk(bias, other, at.col(other, f_other - a + 4, g_other - b + 4))
            arrived(part, p_recv.at[a, b])
    for n in (1, 2, 3):
        arrived(mine, z_send.at[n - 1])
        arrived(own, f_send.at[n - 1])
        for a in range(4):
            arrived(own, g_send.at[a, n - 1])
    for a in range(4):
        for b in range(4):
            arrived(own, p_send.at[a, b])
    exchange_sent(at, msg, in_send)


def attend_kernel(
    bias,
    mask,
    q,
    k,
    v,
    d,
    q_t,
    k_t,
    v_t,
    d_t,
    gate,
    dgate,
    normed,
    w_out,
    w_proj,
    update,
    d_normed,
    proj,
    d_bias,
    bias_t,
    d_bias_t,
    att_t,
    dq_t,
    dk,
    dv,
):
    blocks = [slice(n * C, (n + 1) * C) for n in range(3)]
    negative = (mask[...] - 1.0) * 1e9
    for h in range(H):
        for lanes in blocks:
            bias_t[h, :, lanes] = bias[lanes, h, :].T + negative
    dk[...] = jnp.zeros_like(dk)
    dv[...] = jnp.zeros_like(dv)

    def head(h, carry):
        at_head = pl.multiple_of(h * DH, DH)
        here = pl.ds(at_head, DH)
        lane = lax.div(lax.broadcasted_iota(jnp.int32, (C, C), 1), DH)
        row = lax.div(lax.broadcasted_iota(jnp.int32, (C, C), 0), DH)
        by_lane = (lane == h).astype(F32).astype(BF16)
        by_row = (row == h).astype(F32).astype(BF16)
        for s in range(OWN):
            keys, values = k[s], v[s]
            keys_t, values_t = k_t[s, here, :], v_t[s, here, :]
            dk_sum = dv_sum = None
            for lanes in blocks:
                scores = jnp.dot(keys, q_t[s, :, lanes] * by_row, preferred_element_type=F32)
                scores = scores + bias_t[h, :, lanes]
                exponent = jnp.exp(scores - jnp.max(scores, axis=0, keepdims=True))
                weights = exponent * (1.0 / jnp.sum(exponent, axis=0, keepdims=True))
                weights_b = weights.astype(BF16)
                attended = jnp.dot(values_t, weights_b, preferred_element_type=F32)
                att_t[s, here, lanes] = attended
                delta = jnp.sum(attended * d_t[s, here, lanes].astype(F32), axis=0, keepdims=True)
                d_prob = jnp.dot(values, d_t[s, :, lanes] * by_row, preferred_element_type=F32)
                d_score = weights * (d_prob - delta)
                d_score_b = d_score.astype(BF16)
                if s == 0:
                    d_bias_t[h, :, lanes] = d_score
                else:
                    d_bias_t[h, :, lanes] += d_score
                dq_t[s, here, lanes] = jnp.dot(keys_t, d_score_b, preferred_element_type=F32)
                dv_part = jnp.dot(weights_b, d[s, lanes, :] * by_lane, preferred_element_type=F32)
                dk_part = jnp.dot(d_score_b, q[s, lanes, :] * by_lane, preferred_element_type=F32)
                dv_sum = dv_part if dv_sum is None else dv_sum + dv_part
                dk_sum = dk_part if dk_sum is None else dk_sum + dk_part
            dk[s] += dk_sum
            dv[s] += dv_sum
        return carry

    lax.fori_loop(0, H, head, 0)
    for h in range(H):
        for lanes in blocks:
            d_bias[lanes, h, :] = d_bias_t[h, :, lanes].T

    at = Place()
    for s in range(OWN):
        attended = att_t[s].T
        gated = (gate[s] * attended).astype(BF16)
        pair = mask[...] * mask[pl.ds(at.row0 + s, 1), :]
        update[s] = jnp.dot(gated, w_out[...], preferred_element_type=F32) * pair
        d_proj = jnp.concatenate(
            [dq_t[s].T * DH ** (-0.5), dk[s], dv[s], dgate[s] * attended], axis=1
        ).astype(BF16)
        d_normed[s] = lax.dot_general(d_proj, w_proj[...], NT, preferred_element_type=F32)
        normed_t = normed[s].astype(F32).T.astype(BF16)
        part = jnp.dot(normed_t, d_proj, preferred_element_type=F32)
        if s == 0:
            proj[...] = part
        else:
            proj[...] += part


def reduce_kernel(
    d_bias,
    proj,
    d_normed,
    update,
    standard,
    rstd,
    gain,
    w_bias_t,
    out,
    proj_out,
    ra,
    r2,
    tt,
    r3,
    uu,
    r4,
    r5,
    v5,
    r6,
    v6,
    stage,
    outbox,
    a_send,
    a_recv,
    g_send,
    g_recv,
    f_send,
    f_recv,
    z_send,
    z_recv,
    c_send,
    c_recv,
    w_send,
    w_recv,
    o_send,
    o_recv,
    m_send,
    m_recv,
):
    at = Place()
    e, f, g = at.e, at.f, at.g
    count = greet_common(at)

    def greet_column(n, carry):
        greet((e, at.z, lax.rem(at.c + n, COLS)))
        return carry

    lax.fori_loop(1, COLS, greet_column, 0)

    def greet_source(n, carry):
        z = lax.rem(n, 4) * 2 + e
        core = lax.div(n, 4)

        @pl.when(jnp.logical_not(jnp.logical_and(z == at.z, core == e)))
        def _():
            greet((core, z, at.c))

        return carry

    lax.fori_loop(0, 8, greet_source, 0)
    count = count + (COLS - 1) + 8 - at.stays.astype(jnp.int32)
    pl.semaphore_wait(pltpu.get_barrier_semaphore(), count)

    other = 1 - e
    for b in (1, 2, 3, 0):
        for a in range(4):
            column = at.col(other, g + a, f + b)
            remote(
                d_bias.at[:, other, column],
                ra.at[b, lax.rem(g + a, 4)],
                a_send.at[b, a],
                a_recv.at[b, a],
                at.partner(),
            ).start()

    def rows_of(ref, c):
        return ref.at[pl.ds(pl.multiple_of(c * 8, 8), 8), :]

    def scatter(n, carry):
        t = lax.rem(at.c + n, COLS)
        remote(rows_of(proj, t), r5.at[n], c_send.at[n], c_recv.at[n], (e, at.z, t)).start()
        return carry

    lax.fori_loop(1, COLS, scatter, 0)

    for b in (1, 2, 3, 0):
        for a in range(4):
            ff = lax.rem(f + a, 4)
            arrived(ra.at[b, ff], a_recv.at[b, a])
            ra[b, ff] += d_bias[:, e, at.col(e, f + a, g + b)]
        if b > 0:
            remote(ra.at[b], r2.at[b - 1], g_send.at[b - 1], g_recv.at[b - 1], at.gpeer(b)).start()

    def column_arrived(n, total):
        arrived(r5.at[n], c_recv.at[n])
        return total + r5[n]

    start = proj[pl.ds(pl.multiple_of(at.c * 8, 8), 8), :]
    v5[...] = lax.fori_loop(1, COLS, column_arrived, start)
    worker = e * 4 + at.zz

    def to_all(z, carry):
        here = jnp.logical_and(at.stays, z == at.z)

        @pl.when(here)
        def _():
            pltpu.make_async_copy(v5, r6.at[worker], w_recv.at[worker]).start()

        @pl.when(jnp.logical_not(here))
        def _():
            remote(v5, r6.at[worker], w_send.at[z], w_recv.at[worker], (at.part, z, at.c)).start()

        return carry

    lax.fori_loop(0, 8, to_all, 0)

    for n in (1, 2, 3):
        arrived(r2.at[n - 1], g_recv.at[n - 1])
    for a in (1, 2, 3, 0):
        ff = lax.rem(f + a, 4)
        tt[ff] = (ra[0, ff] + r2[0, ff]) + (r2[1, ff] + r2[2, ff])
        if a > 0:
            remote(tt.at[ff], r3.at[a - 1], f_send.at[a - 1], f_recv.at[a - 1], at.fpeer(a)).start()

    def worker_arrived(n, total):
        arrived(r6.at[n], w_recv.at[n])
        return total + r6[n]

    v6[...] = lax.fori_loop(0, 8, worker_arrived, jnp.zeros((8, 4 * HD), F32))
    own_rows = rows_of(proj_out, at.c)
    pltpu.make_async_copy(v6, own_rows, o_recv.at[0]).start()

    def spread(n, carry):
        t = lax.rem(at.c + n, COLS)
        remote(v6, own_rows, o_send.at[n], o_recv.at[n], (e, at.z, t)).start()
        return carry

    lax.fori_loop(1, COLS, spread, 0)

    for n in (1, 2, 3):
        arrived(r3.at[n - 1], f_recv.at[n - 1])
    uu[...] = (tt[f] + r3[0]) + (r3[1] + r3[2])
    for n in (1, 2, 3):
        there = lax.rem(at.zz + n, 4)
        remote(uu.at[there], r4.at[n - 1], z_send.at[n - 1], z_recv.at[n - 1], at.zpeer(n)).start()
    for n in (1, 2, 3):
        arrived(r4.at[n - 1], z_recv.at[n - 1])
    total = (uu[at.zz] + r4[0]) + (r4[1] + r4[2])

    for s in range(OWN):
        bias_term = lax.dot_general(
            total[s], w_bias_t[...], TN, preferred_element_type=F32, precision=lax.Precision.HIGHEST
        )
        unit = standard[s]
        grad = (d_normed[s] + bias_term) * gain[...]
        mean_grad = jnp.mean(grad, axis=-1, keepdims=True)
        mean_cross = jnp.mean(grad * unit, axis=-1, keepdims=True)
        result = rstd[s] * (grad - mean_grad - unit * mean_cross)
        stage[:, s * WIDTH : (s + 1) * WIDTH, :] = update[s].reshape(COLS, WIDTH, C)
        stage[:, PART + s * WIDTH : PART + (s + 1) * WIDTH, :] = result.reshape(COLS, WIDTH, C)
    outbox[...] = stage[...].astype(BF16)
    exchange_start(at, outbox, out, m_send, m_recv)
    exchange_arrived(out, m_recv)

    def out_arrived(n, carry):
        t = lax.rem(at.c - n + COLS, COLS)
        arrived(rows_of(proj_out, t), o_recv.at[n])
        return carry

    lax.fori_loop(0, COLS, out_arrived, 0)
    for b in range(4):
        for a in range(4):
            arrived(ra.at[0, 0], a_send.at[b, a])
    for n in range(3):
        arrived(r2.at[0], g_send.at[n])
        arrived(r3.at[0], f_send.at[n])
        arrived(r4.at[0], z_send.at[n])

    def column_sent(n, carry):
        arrived(v5, c_send.at[n])
        arrived(v6, o_send.at[n])
        return carry

    lax.fori_loop(1, COLS, column_sent, 0)

    def worker_sent(z, carry):
        @pl.when(jnp.logical_not(jnp.logical_and(at.stays, z == at.z)))
        def _():
            arrived(v5, w_send.at[z])

        return carry

    lax.fori_loop(0, 8, worker_sent, 0)
    exchange_sent(at, outbox, m_send)


def dma(*shape):
    return pltpu.SemaphoreType.DMA(shape)


def vmem(count):
    return [pl.BlockSpec(memory_space=pltpu.VMEM)] * count


def shards(
    pair_act, cotangent, ln_gain, ln_shift, w_proj, gate_bias, w_bias, w_out, residue_mask, valid_length
):
    any_space = pl.BlockSpec(memory_space=pl.ANY)
    positions = lax.axis_index("col") * WIDTH + lax.iota(jnp.int32, WIDTH)
    flags = jnp.where(positions < valid_length[0], residue_mask, 0).astype(BF16)
    msg = jnp.concatenate(
        [
            pair_act.reshape(COLS, PART, C),
            cotangent.reshape(COLS, PART, C),
            jnp.broadcast_to(flags[None, :, None], (COLS, WIDTH, C)),
            jnp.zeros((COLS, INBOX - 2 * PART - WIDTH, C), BF16),
        ],
        axis=1,
    )
    gain = ln_gain.reshape(1, C)
    w_bias_t = w_bias.T
    natural = jax.ShapeDtypeStruct((OWN, N, C), F32)
    natural_b = jax.ShapeDtypeStruct((OWN, N, C), BF16)
    turned_b = jax.ShapeDtypeStruct((OWN, C, N), BF16)
    (bias, normed, standard, rstd, q, k, v, d, q_t, k_t, v_t, d_t, gate, dgate, mask) = pl.pallas_call(
        gather_kernel,
        out_shape=[
            jax.ShapeDtypeStruct((4, 2, COLS, OWN, H, N), F32),
            natural_b,
            natural,
            natural,
            natural_b,
            natural_b,
            natural_b,
            natural_b,
            turned_b,
            turned_b,
            turned_b,
            turned_b,
            natural,
            natural,
            jax.ShapeDtypeStruct((N, C), F32),
        ],
        in_specs=[any_space] + vmem(7),
        out_specs=vmem(15),
        scratch_shapes=[
            pltpu.VMEM((COLS, INBOX, C), BF16),
            dma(COLS),
            dma(COLS),
            dma(3),
            dma(3),
            dma(3),
            dma(3),
            dma(4, 3),
            dma(4, 3),
            dma(4, 4),
            dma(4, 4),
        ],
        compiler_params=pltpu.CompilerParams(
            collective_id=0, has_side_effects=True, vmem_limit_bytes=VMEM_LIMIT
        ),
        name="gather",
    )(
        msg,
        gain,
        ln_shift.reshape(1, C),
        w_proj,
        w_proj[:, : 3 * HD].T,
        gate_bias.reshape(1, HD),
        jnp.concatenate([w_bias_t, jnp.zeros((12, C), BF16)], axis=0),
        w_out,
    )
    update, d_normed, proj, d_bias = pl.pallas_call(
        attend_kernel,
        out_shape=[
            natural,
            natural,
            jax.ShapeDtypeStruct((C, 4 * HD), F32),
            jax.ShapeDtypeStruct((N, H, N), F32),
        ],
        in_specs=vmem(15),
        out_specs=vmem(4),
        scratch_shapes=[
            pltpu.VMEM((H, N, N), F32),
            pltpu.VMEM((H, N, N), F32),
            pltpu.VMEM((OWN, HD, N), F32),
            pltpu.VMEM((OWN, HD, N), F32),
            pltpu.VMEM((OWN, N, HD), F32),
            pltpu.VMEM((OWN, N, HD), F32),
        ],
        compiler_params=pltpu.CompilerParams(vmem_limit_bytes=VMEM_LIMIT),
        name="attend",
    )(bias.reshape(N, H, N), mask, q, k, v, d, q_t, k_t, v_t, d_t, gate, dgate, normed, w_out, w_proj)
    block = (4, OWN, H, N)
    out, proj_out = pl.pallas_call(
        reduce_kernel,
        out_shape=[
            jax.ShapeDtypeStruct((COLS, 2 * PART, C), BF16),
            jax.ShapeDtypeStruct((C, 4 * HD), F32),
        ],
        in_specs=vmem(8),
        out_specs=[any_space, any_space],
        scratch_shapes=[
            pltpu.VMEM((4, 4) + block, F32),
            pltpu.VMEM((3, 4) + block, F32),
            pltpu.VMEM((4,) + block, F32),
            pltpu.VMEM((3,) + block, F32),
            pltpu.VMEM(block, F32),
            pltpu.VMEM((3,) + block[1:], F32),
            pltpu.VMEM((COLS, 8, 4 * HD), F32),
            pltpu.VMEM((8, 4 * HD), F32),
            pltpu.VMEM((8, 8, 4 * HD), F32),
            pltpu.VMEM((8, 4 * HD), F32),
            pltpu.VMEM((COLS, 2 * PART, C), F32),
            pltpu.VMEM((COLS, 2 * PART, C), BF16),
            dma(4, 4),
            dma(4, 4),
            dma(3),
            dma(3),
            dma(3),
            dma(3),
            dma(3),
            dma(3),
            dma(COLS),
            dma(COLS),
            dma(8),
            dma(8),
            dma(COLS),
            dma(COLS),
            dma(COLS),
            dma(COLS),
        ],
        compiler_params=pltpu.CompilerParams(
            collective_id=1, has_side_effects=True, vmem_limit_bytes=VMEM_LIMIT
        ),
        name="reduce",
    )(
        d_bias.reshape((4, 2, COLS, OWN, H, N)),
        proj,
        d_normed,
        update,
        standard,
        rstd,
        gain,
        w_bias_t.astype(F32),
    )
    shape = pair_act.shape
    return (out[:, :PART].reshape(shape), out[:, PART:].reshape(shape), proj_out)


def solution(mesh):
    return jax.shard_map(
        shards,
        mesh=mesh,
        in_specs=(
            P(("complex", "row"), "col", None),
            P(("complex", "row"), "col", None),
            P(),
            P(),
            P(),
            P(),
            P(),
            P(),
            P(("complex", "col")),
            P("complex"),
        ),
        out_specs=(
            P(("complex", "row"), "col", None),
            P(("complex", "row"), "col", None),
            P("complex", None),
        ),
        check_vma=False,
    )
```

time: 626 us -> 126 us (0.20)
  waiting for transfers between devices: 372 us -> 0 us
  Pallas kernels: 0 us -> 116 us
  local copies, waits for them, and re-layouts: 99.6 us -> 5.11 us
  blocking collectives: 51.4 us -> 0 us
  matrix products: 35.3 us -> 0 us
  other arithmetic: 33.2 us -> 3.61 us
  between operations: 17 us -> 1.35 us
  starting transfers between devices: 6.71 us -> 0 us
    psum x3 -> x0, waiting for transfers between devices: 316 us -> none  [the longest x1 207 us: finish(): weight_grad = lax.psum(weight_part, ('row', 'col'))]
    pallas_call x0 -> x3, Pallas kernels: none -> 116 us  [the longest x1 50.1 us: shards(): pl.pallas_call(gather_kernel, out_shape=[jax.ShapeDtypeStruct((4, 2, COLS...]
    reduce_scatter x1 -> x0, waiting for transfers between devices: 39.5 us -> none  [shards(): lax.psum_scatter(d_keyval_part, 'col', scatter_dimension=1, tiled=True)]
    unnamed x1 -> x0, blocking collectives: 31.1 us -> none
    dynamic_update_slice x18 -> x0, local copies, waits for them, and re-layouts: 30.5 us -> none  [attend_blocks(): lax.scan(row_step, jnp.zeros((head_count, col_count, key_count), jnp.floa...]
    dot_general x37 -> x0, matrix products: 25.9 us -> none  [the longest x6 9.77 us: attend(): jnp.einsum('bjhd,bkhd->bhjk', d_four, v_four, preferred_element_type=jnp....]
    all_gather x1 -> x0, blocking collectives: 20.3 us -> none  [shards(): bias_band = lax.all_gather(bias_piece, 'col', axis=2, tiled=True)]
    while x85 -> x0, local copies, waits for them, and re-layouts: 19.7 us -> none
  transfers between devices with their start and end apart: 6 -> 0, of which waited for: 6 -> 0; matrix products, arithmetic and copies ran while one was open for 3% -> 0% of each run, Pallas kernels for 0% -> 0%
where the time goes in v1:
time: 126 us
  Pallas kernels  116 us (92%)
  local copies, waits for them, and re-layouts  5.11 us (4%)
  other arithmetic  3.61 us (3%)
  between operations  1.35 us (1%)
    pallas_call x1, Pallas kernels, shards(): pl.pallas_call(gather_kernel, out_shape=[jax.ShapeDtypeStruct((4, 2, COLS...  50.1 us
    pallas_call x1, Pallas kernels, shards(): pl.pallas_call(reduce_kernel, out_shape=[jax.ShapeDtypeStruct((COLS, 2 *...  39.3 us
    pallas_call x1, Pallas kernels, shards(): pl.pallas_call(attend_kernel, out_shape=[natural, natural, jax.ShapeDtype...  26.5 us

profile of v1, /device:TPU:1, one launch (start us, length us, event | category | flops | bytes accessed | tf_op | source)
XLA Modules:
  0.0 126.0 jit_solution(2695051210220864339)
XLA Ops:
  0.6 0.0 slice-start
  0.6 0.0 copy-start
  1.3 0.7 fusion
  2.0 0.1 pad.3.clone
  2.1 0.1 pad.4.clone
  2.2 2.4 %maximum_maximum_fusion.msg = bf16[16,176,128]{2,1,0:T(8,128)(2,1)} fusion(bf16[16,72,128]{2,1,0:T(8,128)(2,1)} %bitcast.17, bf16[16,72,128]{2,1,0:T(8,128)(2,1)} %bitcast.18, bf16[176]{0:T(256)(128)(2,1)S(1)} %pad.4.clone, bf16[176]{0:T(256)(128)(2,1)S(1)} %pad.3.clone), kind=kLoop, calls=%fused_computation | loop fusion | flops 2883584 | bytes 1311424 | tf_op jit(solution)/shard_map/concatenate | solution.py:567
  4.5 0.0 slice-done
  4.5 0.8 copy.14
  5.3 0.0 copy-done
  5.3 0.6 concatenate.7.w_bias_t
  5.9 50.1 %gather.1 = (f32[4,2,16,3,4,384]{5,4,3,2,1,0:T(4,128)}, bf16[3,384,128]{2,1,0:T(8,128)(2,1)}, f32[3,384,128]{2,1,0:T(8,128)}, f32[3,384,128]{2,1,0:T(8,128)}, bf...) custom-call(bf16[16,176,128]{2,1,0:T(8,128)(2,1)} %maximum_maximum_f, ...), custom_call_target="tpu_custom_call" | custom-call | tf_op jit(solution)/shard_map/gather/pallas_call | solution.py:581
  56.0 26.5 %attend.1 = (f32[3,384,128]{2,1,0:T(8,128)}, f32[3,384,128]{2,1,0:T(8,128)}, f32[128,512]{1,0:T(8,128)}, f32[384,4,384]{2,1,0:T(4,128)}) custom-call(f32[384,4,384]{2,1,0:T(4,128)} %bitcast.14, f32[384,128]{1,0:T(8,128)} %get-tuple-element.25.mask, bf16[3,384,128]{2,1,0:T(8,128)(2,1)} %get-tuple-element.26.q, bf16[3,384,128]{2,1,0:T(8,128)(2,1)} %get-tuple-element.27.k, ...), custom_call_target="tpu_custom_call" | custom-call | tf_op jit(solution)/shard_map/attend/pallas_call | solution.py:629
  82.5 0.6 bitcast_convert_fusion.w_bias_t
  83.1 39.3 %reduce.1 = (bf16[16,144,128]{2,1,0:T(8,128)(2,1)}, f32[128,512]{1,0:T(8,128)}) custom-call(f32[4,2,16,3,4,384]{5,4,3,2,1,0:T(4,128)} %bitcast.15, f32[128,512]{1,0:T(8,128)} %get-tuple-element.38.proj, f32[3,384,128]{2,1,0:T(8,128)} %get-tuple-element.39.d_normed, f32[3,384,128]{2,1,0:T(8,128)} %get-tuple-element.40.update, ...), custom_call_target="tpu_custom_call" | custom-call | tf_op jit(solution)/shard_map/reduce/pallas_call | solution.py:651
  122.4 1.9 %fusion.1 = (bf16[16,72,128]{2,1,0:T(8,128)(2,1)}, bf16[16,72,128]{2,1,0:T(8,128)(2,1)}) fusion(bf16[16,144,128]{2,1,0:T(8,128)(2,1)} %get-tuple-element.43), kind=kLoop, calls=%fused_computation.4 | loop fusion | bytes 1179648 | tf_op jit(solution)/shard_map/slice | solution.py:704
  124.3 1.7 %copy.17 = f32[128,512]{1,0:T(8,128)} copy(f32[128,512]{1,0:T(8,128)} %get-tuple-element.52) | data formatting | bytes 524288
  (1 shorter events, 0.0 us)
Async XLA Ops:
  0.6 3.9 %slice-start = ((bf16[128,512]{1,0:T(8,128)(2,1)}), bf16[128,384]{1,0:T(8,128)(2,1)S(1)}, s32[]{:S(2)}) async-start(bf16[128,512]{1,0:T(8,128)(2,1)} %w_proj.3), calls=%async_computation | async-start | bytes 196608 | tf_op jit(solution)/shard_map/slice | solution.py:624
  0.6 4.6 %copy-start = (bf16[128,4]{0,1:T(4,128)(2,1)S(1)}, bf16[128,4]{0,1:T(4,128)(2,1)}, u32[]{:S(2)}) copy-start(bf16[128,4]{0,1:T(4,128)(2,1)} %param.16) | copy-start | bytes 3076

commit v2 on v0

v2 whole, which is shorter than its diff:
```python
import jax
import jax.numpy as jnp
from jax import lax
from jax.experimental import pallas as pl
from jax.experimental.pallas import tpu as pltpu
from jax.sharding import PartitionSpec as P

MESH = pl.DeviceIdType.MESH
F32 = jnp.float32
BF16 = jnp.bfloat16
N = 384
C = 128
H = 4
DH = 32
HD = H * DH
COLS = 16
ROWS = 8
WIDTH = N // COLS
TALL = N // ROWS
OWN = 3
PART = OWN * WIDTH
PADDED = 80
SLOT = 64
PAIR = 2 * SLOT
SCALE = DH ** (-0.5)
VMEM_LIMIT = 60 * 1024 * 1024
NT = (((1,), (1,)), ((), ()))


class Place:
    def __init__(self):
        self.e = lax.axis_index("complex")
        self.z = lax.axis_index("row")
        self.c = lax.axis_index("col")
        self.part = lax.rem(self.z, 2)
        self.zz = lax.div(self.z, 2)
        self.stays = self.part == self.e
        self.row0 = (self.zz * 2 + self.e) * TALL + self.c * OWN

    def swapped(self, c):
        return (self.part, self.zz * 2 + self.e, c)

    def plane(self, n):
        return (self.e, self.z, lax.rem(self.c + n, COLS))

    def partner(self):
        return (1 - self.e, self.z, self.c)

    def worker(self, core, zz):
        return (core, zz * 2 + self.e, self.c)

    def home(self, z):
        return (self.part, z, self.c)

    def is_worker(self, core, zz):
        return jnp.logical_and(self.stays, jnp.logical_and(core == self.e, zz == self.zz))

    def is_home(self, z):
        return jnp.logical_and(self.stays, z == self.z)


def remote(src, dst, send, recv, device):
    return pltpu.make_async_remote_copy(
        src_ref=src, dst_ref=dst, send_sem=send, recv_sem=recv, device_id=device, device_id_type=MESH
    )


def arrived(ref, sem):
    pltpu.make_async_copy(ref, ref, sem).wait()


def send_or_copy(here, src, dst, send, recv, device):
    @pl.when(here)
    def _():
        pltpu.make_async_copy(src, dst, recv).start()

    @pl.when(jnp.logical_not(here))
    def _():
        remote(src, dst, send, recv, device).start()


def greet(device):
    pl.semaphore_signal(pltpu.get_barrier_semaphore(), inc=1, device_id=device, device_id_type=MESH)


def greet_all(at):
    def plane(n, carry):
        greet(at.plane(n))
        return carry

    lax.fori_loop(1, COLS, plane, 0)

    def worker(n, carry):
        core, zz = lax.div(n, 4), lax.rem(n, 4)

        @pl.when(jnp.logical_not(at.is_worker(core, zz)))
        def _():
            greet(at.worker(core, zz))

        return carry

    lax.fori_loop(0, 8, worker, 0)

    def home(n, carry):
        greet(at.home(n * 2 + 1 - at.e))
        return carry

    lax.fori_loop(0, 4, home, 0)

    @pl.when(jnp.logical_not(at.stays))
    def _():
        def column(n, carry):
            greet(at.swapped(n))
            return carry

        lax.fori_loop(0, COLS, column, 0)

    return jnp.where(at.stays, COLS - 1 + 7 + 4, COLS - 1 + 8 + 4 + COLS)


def exchange_start(at, source, landing, send, recv):
    def column(n, carry):
        t = lax.rem(at.c + n, COLS)
        here = jnp.logical_and(n == 0, at.stays)
        send_or_copy(here, source.at[t], landing.at[at.c], send.at[t], recv.at[at.c], at.swapped(t))
        return carry

    lax.fori_loop(0, COLS, column, 0)


def exchange_arrived(landing, recv):
    def column(n, carry):
        arrived(landing.at[n], recv.at[n])
        return carry

    lax.fori_loop(0, COLS, column, 0)


def exchange_sent(at, source, send):
    def column(n, carry):
        t = lax.rem(at.c + n, COLS)

        @pl.when(jnp.logical_or(n > 0, jnp.logical_not(at.stays)))
        def _():
            arrived(source.at[t], send.at[t])

        return carry

    lax.fori_loop(0, COLS, column, 0)


def repeat_heads(w_bias):
    wide = w_bias[...].astype(F32)
    lane = lax.div(lax.broadcasted_iota(jnp.int32, (C, H * SLOT), 1), SLOT)
    total = jnp.zeros((C, H * SLOT), F32)
    for h in range(H):
        total = jnp.where(lane == h, wide[:, h : h + 1], total)
    return total.astype(BF16)


def only_row(repeated, i):
    lane = lax.rem(lax.broadcasted_iota(jnp.int32, (C, H * SLOT), 1), SLOT)
    return repeated * (lane == i).astype(F32).astype(BF16)


def standardize(values):
    centre = values - jnp.mean(values, axis=-1, keepdims=True)
    inverse = lax.rsqrt(jnp.mean(centre * centre, axis=-1, keepdims=True) + 1e-5)
    return centre * inverse, jnp.broadcast_to(inverse, values.shape)


def norm_backward(grad, unit, inverse):
    mean_grad = jnp.mean(grad, axis=-1, keepdims=True)
    mean_cross = jnp.mean(grad * unit, axis=-1, keepdims=True)
    return inverse * (grad - mean_grad - unit * mean_cross)


MAIN_SCRATCH = dict(
    m1=((COLS, PADDED, C), BF16),
    m2=((COLS, PART + WIDTH, C), BF16),
    in1=((COLS, PADDED, C), BF16),
    in2=((COLS, PART + WIDTH, C), BF16),
    w_proj_t=((3 * HD, C), BF16),
    w_rep=((C, H * SLOT), BF16),
    home_rows=((TALL, WIDTH, C), F32),
    zpack=((2, WIDTH, PAIR), F32),
    zin=((ROWS, WIDTH, PAIR), F32),
    bias=((H, COLS, WIDTH, N), F32),
    d_bias=((H, COLS, WIDTH, N), F32),
    d_other=((2, COLS, WIDTH, N), F32),
    d_plane=((2, COLS, WIDTH, N), F32),
    zout=((ROWS, WIDTH, PAIR), F32),
    hin=((2, 4, WIDTH, PAIR), F32),
    mask=((N, C), F32),
    normed=((OWN, N, C), BF16),
    unit=((OWN, N, C), F32),
    rstd=((OWN, N, C), F32),
    q=((OWN, N, C), BF16),
    k=((OWN, N, C), BF16),
    v=((OWN, N, C), BF16),
    d=((OWN, N, C), BF16),
    q_t=((OWN, C, N), BF16),
    k_t=((OWN, C, N), BF16),
    v_t=((OWN, C, N), BF16),
    d_t=((OWN, C, N), BF16),
    gate=((OWN, N, C), F32),
    dgate=((OWN, N, C), F32),
    att_t=((OWN, HD, N), F32),
    dq_t=((OWN, HD, N), F32),
    dk=((OWN, N, HD), F32),
    dv=((OWN, N, HD), F32),
    proj=((C, 4 * HD), F32),
    r5=((COLS, 8, 4 * HD), F32),
    v5=((8, 4 * HD), F32),
    r6=((8, 8, 4 * HD), F32),
    v6=((8, 4 * HD), F32),
    stage_u=((COLS, PADDED, C), F32),
    stage_a=((COLS, PADDED, C), F32),
    out_u=((COLS, PADDED, C), BF16),
    out_a=((COLS, PADDED, C), BF16),
)
MAIN_SEMS = dict(
    in1=(COLS,),
    in2=(COLS,),
    z=(8,),
    plane=(2, COLS),
    partner=(2,),
    back=(2,),
    d_plane=(2, COLS),
    dz=(8,),
    p1=(COLS,),
    p2=(8,),
    p3=(COLS,),
    u=(COLS,),
    a=(COLS,),
)
MAIN_IN = 9
MAIN_OUT = 6


class Names:
    pass


def main_kernel(*refs):
    (pair, cot, flags, gain, shift, w_proj, gate_bias, w_bias, w_out) = refs[:MAIN_IN]
    (land_u, land_a, proj_out, h_sum, home_unit, home_rstd) = refs[MAIN_IN : MAIN_IN + MAIN_OUT]
    rest = refs[MAIN_IN + MAIN_OUT :]
    m, send, recv = Names(), Names(), Names()
    for name, ref in zip(MAIN_SCRATCH, rest):
        setattr(m, name, ref)
    rest = rest[len(MAIN_SCRATCH) :]
    for name, ref in zip(MAIN_SEMS, rest):
        setattr(send, name, ref)
    for name, ref in zip(MAIN_SEMS, rest[len(MAIN_SEMS) :]):
        setattr(recv, name, ref)
    at = Place()
    e = at.e
    count = greet_all(at)

    m.m1[...] = jnp.concatenate(
        [pair[...].astype(F32).reshape(COLS, PART, C), jnp.zeros((COLS, PADDED - PART, C), F32)], axis=1
    ).astype(BF16)
    m.m2[...] = jnp.concatenate(
        [
            cot[...].astype(F32).reshape(COLS, PART, C),
            jnp.broadcast_to(flags[...][None], (COLS, WIDTH, C)),
        ],
        axis=1,
    ).astype(BF16)
    pl.semaphore_wait(pltpu.get_barrier_semaphore(), count)
    exchange_start(at, m.m1, m.in1, send.in1, recv.in1)
    exchange_start(at, m.m2, m.in2, send.in2, recv.in2)

    m.w_rep[...] = repeat_heads(w_bias)
    unit, inverse = standardize(pair[...].astype(F32).reshape(TALL * WIDTH, C))
    home_unit[...] = unit.reshape(TALL, WIDTH, C)
    home_rstd[...] = inverse.reshape(TALL, WIDTH, C)
    m.home_rows[...] = (unit * gain[...] + shift[...]).reshape(TALL, WIDTH, C)

    def home_bias(n, total):
        for i in range(8):
            rows = m.home_rows[n * 8 + i].astype(BF16)
            total = total + jnp.dot(rows, only_row(m.w_rep[...], n * 8 + i), preferred_element_type=F32)
        return total

    packed = lax.fori_loop(0, TALL // 8, home_bias, jnp.zeros((WIDTH, H * SLOT), F32))
    negative = (flags[...] - 1.0) * 1e9
    m.zpack[0] = packed[:, :PAIR] + negative
    m.zpack[1] = packed[:, PAIR:] + negative

    def to_workers(n, carry):
        core, zz = lax.div(n, 4), lax.rem(n, 4)
        send_or_copy(
            at.is_worker(core, zz),
            m.zpack.at[core],
            m.zin.at[at.z],
            send.z.at[n],
            recv.z.at[at.z],
            at.worker(core, zz),
        )
        return carry

    lax.fori_loop(0, 8, to_workers, 0)

    m.w_proj_t[...] = w_proj[:, : 3 * HD].astype(F32).T.astype(BF16)
    m.d_bias[...] = jnp.zeros_like(m.d_bias)
    m.dk[...] = jnp.zeros_like(m.dk)
    m.dv[...] = jnp.zeros_like(m.dv)
    exchange_arrived(m.in1, recv.in1)

    for s in range(OWN):
        values = m.in1[:, s * WIDTH : (s + 1) * WIDTH, :].astype(F32).reshape(N, C)
        unit, inverse = standardize(values)
        m.unit[s] = unit
        m.rstd[s] = inverse
        m.normed[s] = (unit * gain[...] + shift[...]).astype(BF16)

    for z in range(ROWS):
        arrived(m.zin.at[z], recv.z.at[z])
    for hh in range(2):
        head = e * 2 + hh
        m.bias[head, at.c] = jnp.concatenate(
            [m.zin[z][:, hh * SLOT : hh * SLOT + TALL] for z in range(ROWS)], axis=1
        )
        mine = m.bias.at[head, at.c]

        def to_plane(n, carry):
            remote(mine, mine, send.plane.at[hh, n], recv.plane.at[hh, n], at.plane(n)).start()
            return carry

        lax.fori_loop(1, COLS, to_plane, 0)

    for s in range(OWN):
        rows = m.normed[s]
        flat = jnp.dot(rows, w_proj[...], preferred_element_type=F32)
        m.q[s] = (flat[:, :HD] * SCALE).astype(BF16)
        m.k[s] = flat[:, HD : 2 * HD].astype(BF16)
        m.v[s] = flat[:, 2 * HD : 3 * HD].astype(BF16)
        m.gate[s] = jax.nn.sigmoid(flat[:, 3 * HD :] + gate_bias[...])
        flat_t = lax.dot_general(m.w_proj_t[...], rows, NT, preferred_element_type=F32)
        m.q_t[s] = (flat_t[:HD] * SCALE).astype(BF16)
        m.k_t[s] = flat_t[HD : 2 * HD].astype(BF16)
        m.v_t[s] = flat_t[2 * HD : 3 * HD].astype(BF16)

    exchange_arrived(m.in2, recv.in2)
    m.mask[...] = m.in2[:, PART : PART + WIDTH, :].astype(F32).reshape(N, C)
    for s in range(OWN):
        values = m.in2[:, s * WIDTH : (s + 1) * WIDTH, :].astype(F32).reshape(N, C)
        pair_mask = m.mask[...] * m.mask[pl.ds(at.row0 + s, 1), :]
        d_out = jnp.where(pair_mask > 0, values, 0.0).astype(BF16)
        d_gated = lax.dot_general(d_out, w_out[...], NT, preferred_element_type=F32)
        gates = m.gate[s]
        d_attn = d_gated * gates
        m.d[s] = d_attn.astype(BF16)
        m.d_t[s] = d_attn.T.astype(BF16)
        m.dgate[s] = d_attn * (1.0 - gates)

    def own_bias_arrived(hh):
        head = e * 2 + hh

        def from_plane(n, carry):
            arrived(m.bias.at[head, lax.rem(at.c - n + COLS, COLS)], recv.plane.at[hh, n])
            return carry

        lax.fori_loop(1, COLS, from_plane, 0)
        whole = m.bias.at[head]
        remote(whole, whole, send.partner.at[hh], recv.partner.at[hh], at.partner()).start()

    def other_bias_arrived(hh):
        arrived(m.bias.at[(1 - e) * 2 + hh], recv.partner.at[hh])

    def attend(h):
        here = pl.ds(pl.multiple_of(h * DH, DH), DH)
        lane = lax.div(lax.broadcasted_iota(jnp.int32, (C, C), 1), DH)
        row = lax.div(lax.broadcasted_iota(jnp.int32, (C, C), 0), DH)
        by_lane = (lane == h).astype(F32).astype(BF16)
        by_row = (row == h).astype(F32).astype(BF16)

        def one_row(s, carry):
            keys, values = m.k[s], m.v[s]
            keys_t, values_t = m.k_t[s, here, :], m.v_t[s, here, :]
            dk_sum = dv_sum = None
            for n in range(3):
                lanes = slice(n * C, (n + 1) * C)
                scores = jnp.dot(keys, m.q_t[s, :, lanes] * by_row, preferred_element_type=F32)
                scores = scores + m.bias[h, :, :, lanes].reshape(N, C)
                exponent = jnp.exp(scores - jnp.max(scores, axis=0, keepdims=True))
                weights = exponent * (1.0 / jnp.sum(exponent, axis=0, keepdims=True))
                weights_b = weights.astype(BF16)
                attended = jnp.dot(values_t, weights_b, preferred_element_type=F32)
                m.att_t[s, here, lanes] = attended
                delta = jnp.sum(attended * m.d_t[s, here, lanes].astype(F32), axis=0, keepdims=True)
                d_prob = jnp.dot(values, m.d_t[s, :, lanes] * by_row, preferred_element_type=F32)
                d_score = weights * (d_prob - delta)
                d_score_b = d_score.astype(BF16)
                m.d_bias[h, :, :, lanes] += d_score.reshape(COLS, WIDTH, C)
                m.dq_t[s, here, lanes] = jnp.dot(keys_t, d_score_b, preferred_element_type=F32)
                dv_part = jnp.dot(weights_b, m.d[s, lanes, :] * by_lane, preferred_element_type=F32)
                dk_part = jnp.dot(d_score_b, m.q[s, lanes, :] * by_lane, preferred_element_type=F32)
                dv_sum = dv_part if dv_sum is None else dv_sum + dv_part
                dk_sum = dk_part if dk_sum is None else dk_sum + dk_part
            m.dk[s] += dk_sum
            m.dv[s] += dv_sum
            return carry

        lax.fori_loop(0, OWN, one_row, 0)

    def to_other(hh):
        head = (1 - e) * 2 + hh
        remote(m.d_bias.at[head], m.d_other.at[hh], send.back.at[hh], recv.back.at[hh], at.partner()).start()

    def scatter_plane(hh):
        head = e * 2 + hh
        arrived(m.d_other.at[hh], recv.back.at[hh])
        m.d_bias[head] += m.d_other[hh]

        def to_plane(n, carry):
            remote(
                m.d_bias.at[head, lax.rem(at.c + n, COLS)],
                m.d_plane.at[hh, n],
                send.d_plane.at[hh, n],
                recv.d_plane.at[hh, n],
                at.plane(n),
            ).start()
            return carry

        lax.fori_loop(1, COLS, to_plane, 0)

    def plane_sum(hh):
        def from_plane(n, total):
            arrived(m.d_plane.at[hh, n], recv.d_plane.at[hh, n])
            return total + m.d_plane[hh, n]

        return lax.fori_loop(1, COLS, from_plane, m.d_bias[e * 2 + hh, at.c])

    own_bias_arrived(0)
    attend(e * 2)
    own_bias_arrived(1)
    other_bias_arrived(0)
    attend(2 - e * 2)
    to_other(0)
    other_bias_arrived(1)
    attend(3 - e * 2)
    to_other(1)
    scatter_plane(0)
    attend(e * 2 + 1)
    scatter_plane(1)

    for s in range(OWN):
        attended = m.att_t[s].T
        gated = (m.gate[s] * attended).astype(BF16)
        pair_mask = m.mask[...] * m.mask[pl.ds(at.row0 + s, 1), :]
        update = jnp.dot(gated, w_out[...], preferred_element_type=F32) * pair_mask
        d_proj = jnp.concatenate(
            [m.dq_t[s].T * SCALE, m.dk[s], m.dv[s], m.dgate[s] * attended], axis=1
        ).astype(BF16)
        d_normed = lax.dot_general(d_proj, w_proj[...], NT, preferred_element_type=F32)
        result = norm_backward(d_normed * gain[...], m.unit[s], m.rstd[s])
        m.stage_u[:, s * WIDTH : (s + 1) * WIDTH, :] = update.reshape(COLS, WIDTH, C)
        m.stage_a[:, s * WIDTH : (s + 1) * WIDTH, :] = result.reshape(COLS, WIDTH, C)
        normed_t = m.normed[s].astype(F32).T.astype(BF16)
        share = jnp.dot(normed_t, d_proj, preferred_element_type=F32)
        if s == 0:
            m.proj[...] = share
        else:
            m.proj[...] += share
    pad = jnp.zeros((COLS, PADDED - PART, C), F32)
    m.stage_u[:, PART:, :] = pad
    m.stage_a[:, PART:, :] = pad
    m.out_u[...] = m.stage_u[...].astype(BF16)
    m.out_a[...] = m.stage_a[...].astype(BF16)

    def rows_of(ref, c):
        return ref.at[pl.ds(pl.multiple_of(c * 8, 8), 8), :]

    def scatter_proj(n, carry):
        t = lax.rem(at.c + n, COLS)
        remote(rows_of(m.proj, t), m.r5.at[n], send.p1.at[n], recv.p1.at[n], at.plane(n)).start()
        return carry

    lax.fori_loop(1, COLS, scatter_proj, 0)
    exchange_start(at, m.out_u, land_u, send.u, recv.u)
    exchange_start(at, m.out_a, land_a, send.a, recv.a)

    halves = [plane_sum(0), plane_sum(1)]
    blank = jnp.zeros((WIDTH, SLOT - TALL), F32)
    for z in range(ROWS):
        mine = slice(z * TALL, (z + 1) * TALL)
        m.zout[z] = jnp.concatenate([halves[0][:, mine], blank, halves[1][:, mine], blank], axis=1)

    def to_homes(z, carry):
        send_or_copy(
            at.is_home(z),
            m.zout.at[z],
            m.hin.at[e, at.zz],
            send.dz.at[z],
            recv.dz.at[e * 4 + at.zz],
            at.home(z),
        )
        return carry

    lax.fori_loop(0, ROWS, to_homes, 0)

    def proj_arrived(n, total):
        arrived(m.r5.at[n], recv.p1.at[n])
        return total + m.r5[n]

    m.v5[...] = lax.fori_loop(1, COLS, proj_arrived, m.proj[pl.ds(pl.multiple_of(at.c * 8, 8), 8), :])

    def proj_to_homes(z, carry):
        slot = e * 4 + at.zz
        send_or_copy(at.is_home(z), m.v5, m.r6.at[slot], send.p2.at[z], recv.p2.at[slot], at.home(z))
        return carry

    lax.fori_loop(0, ROWS, proj_to_homes, 0)

    def share_arrived(n, total):
        arrived(m.r6.at[n], recv.p2.at[n])
        return total + m.r6[n]

    m.v6[...] = lax.fori_loop(0, 8, share_arrived, jnp.zeros((8, 4 * HD), F32))
    own_rows = rows_of(proj_out, at.c)
    pltpu.make_async_copy(m.v6, own_rows, recv.p3.at[0]).start()

    def spread(n, carry):
        remote(m.v6, own_rows, send.p3.at[n], recv.p3.at[n], at.plane(n)).start()
        return carry

    lax.fori_loop(1, COLS, spread, 0)

    for core in range(2):
        for zz in range(4):
            arrived(m.hin.at[core, zz], recv.dz.at[core * 4 + zz])
        lanes = slice(core * PAIR, (core + 1) * PAIR)
        h_sum[:, lanes] = (m.hin[core, 0] + m.hin[core, 1]) + (m.hin[core, 2] + m.hin[core, 3])
    exchange_arrived(land_u, recv.u)
    exchange_arrived(land_a, recv.a)

    def out_arrived(n, carry):
        arrived(rows_of(proj_out, lax.rem(at.c - n + COLS, COLS)), recv.p3.at[n])
        return carry

    lax.fori_loop(0, COLS, out_arrived, 0)

    def column_sent(n, carry):
        for hh in range(2):
            arrived(m.bias.at[0, 0], send.plane.at[hh, n])
            arrived(m.d_bias.at[0, 0], send.d_plane.at[hh, n])
        arrived(m.v5, send.p1.at[n])
        arrived(m.v6, send.p3.at[n])
        return carry

    lax.fori_loop(1, COLS, column_sent, 0)

    def column_group_sent(n, carry):
        @pl.when(jnp.logical_not(at.is_worker(lax.div(n, 4), lax.rem(n, 4))))
        def _():
            arrived(m.zpack.at[0], send.z.at[n])

        @pl.when(jnp.logical_not(at.is_home(n)))
        def _():
            arrived(m.zout.at[0], send.dz.at[n])
            arrived(m.v5, send.p2.at[n])

        return carry

    lax.fori_loop(0, 8, column_group_sent, 0)
    for hh in range(2):
        arrived(m.bias.at[0], send.partner.at[hh])
        arrived(m.d_bias.at[0], send.back.at[hh])
    exchange_sent(at, m.m1, send.in1)
    exchange_sent(at, m.m2, send.in2)
    exchange_sent(at, m.out_u, send.u)
    exchange_sent(at, m.out_a, send.a)


def finish_kernel(
    land_u, land_a, proj_in, h_sum, unit, rstd, gain, w_bias, update, pair_grad, proj_out, w_rep, split, share
):
    proj_out[...] = proj_in[...]
    update[...] = land_u[:, :PART, :].astype(F32).reshape(TALL, WIDTH, C).astype(BF16)
    share[...] = land_a[:, :PART, :].astype(F32).reshape(TALL, WIDTH, C)
    w_rep[...] = repeat_heads(w_bias)
    total = h_sum[...]
    for n in range(3):
        term = total.astype(BF16).astype(F32)
        split[n * WIDTH : (n + 1) * WIDTH, :] = term
        total = total - term

    def rows(n, carry):
        terms = split[...].astype(BF16)
        for inner in range(8):
            i = n * 8 + inner
            parts = lax.dot_general(terms, only_row(w_rep[...], i), NT, preferred_element_type=F32)
            grad = (parts[2 * WIDTH :] + parts[WIDTH : 2 * WIDTH]) + parts[:WIDTH]
            result = norm_backward(grad * gain[...], unit[i], rstd[i])
            pair_grad[i] = (share[i] + result).astype(BF16)
        return carry

    lax.fori_loop(0, TALL // 8, rows, 0)


def vmem(count):
    return [pl.BlockSpec(memory_space=pltpu.VMEM)] * count


def shards(
    pair_act, cotangent, ln_gain, ln_shift, w_proj, gate_bias, w_bias, w_out, residue_mask, valid_length
):
    any_space = pl.BlockSpec(memory_space=pl.ANY)
    positions = lax.axis_index("col") * WIDTH + lax.iota(jnp.int32, WIDTH)
    flags = jnp.where(positions < valid_length[0], residue_mask, 0).astype(F32)
    gain = ln_gain.reshape(1, C)
    sems = [pltpu.SemaphoreType.DMA(shape) for shape in MAIN_SEMS.values()]
    landing = jax.ShapeDtypeStruct((COLS, PADDED, C), BF16)
    block = jax.ShapeDtypeStruct(pair_act.shape, F32)
    proj_shape = jax.ShapeDtypeStruct((C, 4 * HD), F32)
    land_u, land_a, proj, h_sum, unit, rstd = pl.pallas_call(
        main_kernel,
        out_shape=[
            landing,
            landing,
            proj_shape,
            jax.ShapeDtypeStruct((WIDTH, H * SLOT), F32),
            block,
            block,
        ],
        in_specs=vmem(MAIN_IN),
        out_specs=[any_space] * 3 + vmem(3),
        scratch_shapes=[pltpu.VMEM(shape, dtype) for shape, dtype in MAIN_SCRATCH.values()] + sems + sems,
        compiler_params=pltpu.CompilerParams(
            collective_id=0, has_side_effects=True, vmem_limit_bytes=VMEM_LIMIT
        ),
        name="main",
    )(
        pair_act,
        cotangent,
        jnp.broadcast_to(flags[:, None], (WIDTH, C)),
        gain,
        ln_shift.reshape(1, C),
        w_proj,
        gate_bias.reshape(1, HD),
        w_bias,
        w_out,
    )
    result = jax.ShapeDtypeStruct(pair_act.shape, BF16)
    return pl.pallas_call(
        finish_kernel,
        out_shape=[result, result, proj_shape],
        in_specs=vmem(8),
        out_specs=vmem(3),
        scratch_shapes=[
            pltpu.VMEM((C, H * SLOT), BF16),
            pltpu.VMEM((3 * WIDTH, H * SLOT), F32),
            pltpu.VMEM(pair_act.shape, F32),
        ],
        compiler_params=pltpu.CompilerParams(vmem_limit_bytes=VMEM_LIMIT),
        name="finish",
    )(land_u, land_a, proj, h_sum, unit, rstd, gain, w_bias)


def solution(mesh):
    return jax.shard_map(
        shards,
        mesh=mesh,
        in_specs=(
            P(("complex", "row"), "col", None),
            P(("complex", "row"), "col", None),
            P(),
            P(),
            P(),
            P(),
            P(),
            P(),
            P(("complex", "col")),
            P("complex"),
        ),
        out_specs=(
            P(("complex", "row"), "col", None),
            P(("complex", "row"), "col", None),
            P("complex", None),
        ),
        check_vma=False,
    )
```

time: 626 us -> 100 us (0.16)
  waiting for transfers between devices: 372 us -> 0 us
  local copies, waits for them, and re-layouts: 99.6 us -> 2.06 us
  Pallas kernels: 0 us -> 96.5 us
  blocking collectives: 51.4 us -> 0 us
  matrix products: 35.3 us -> 0 us
  other arithmetic: 33.2 us -> 0.01 us
  between operations: 17 us -> 1.3 us
  starting transfers between devices: 6.71 us -> 0 us
    psum x3 -> x0, waiting for transfers between devices: 316 us -> none  [the longest x1 207 us: finish(): weight_grad = lax.psum(weight_part, ('row', 'col'))]
    pallas_call x0 -> x2, Pallas kernels: none -> 96.5 us  [the longest x1 91.5 us: shards(): pl.pallas_call(main_kernel, out_shape=[landing, landing, proj_shape, jax....]
    reduce_scatter x1 -> x0, waiting for transfers between devices: 39.5 us -> none  [shards(): lax.psum_scatter(d_keyval_part, 'col', scatter_dimension=1, tiled=True)]
    unnamed x1 -> x0, blocking collectives: 31.1 us -> none
    dynamic_update_slice x18 -> x0, local copies, waits for them, and re-layouts: 30.5 us -> none  [attend_blocks(): lax.scan(row_step, jnp.zeros((head_count, col_count, key_count), jnp.floa...]
    dot_general x37 -> x0, matrix products: 25.9 us -> none  [the longest x6 9.77 us: attend(): jnp.einsum('bjhd,bkhd->bhjk', d_four, v_four, preferred_element_type=jnp....]
    all_gather x1 -> x0, blocking collectives: 20.3 us -> none  [shards(): bias_band = lax.all_gather(bias_piece, 'col', axis=2, tiled=True)]
    while x85 -> x0, local copies, waits for them, and re-layouts: 19.7 us -> none
  transfers between devices with their start and end apart: 6 -> 0, of which waited for: 6 -> 0; matrix products, arithmetic and copies ran while one was open for 3% -> 0% of each run, Pallas kernels for 0% -> 0%
where the time goes in v2:
time: 100 us; the launch traced here: 99.8 us
  Pallas kernels  96.5 us (96%)
  local copies, waits for them, and re-layouts  2.06 us (2%)
  between operations  1.3 us (1%)
    pallas_call x1, Pallas kernels, shards(): pl.pallas_call(main_kernel, out_shape=[landing, landing, proj_shape, jax....  91.5 us
    pallas_call x1, Pallas kernels, shards(): pl.pallas_call(finish_kernel, out_shape=[result, result, proj_shape], in_...  4.98 us

profile of v2, /device:TPU:1, one launch (start us, length us, event | category | flops | bytes accessed | tf_op | source)
XLA Modules:
  0.0 99.8 jit_solution(16534044879248325621)
XLA Ops:
  1.3 0.0 copy-start.1
  1.3 0.6 copy-done.1
  1.9 0.0 copy-start
  1.9 0.7 broadcast_in_dim.11.refs_2_
  2.6 0.0 copy-done
  2.6 0.7 copy.13.refs_7_.w_bias
  3.4 91.5 %main.1 = (bf16[16,80,128]{2,1,0:T(8,128)(2,1)}, bf16[16,80,128]{2,1,0:T(8,128)(2,1)}, f32[128,512]{1,0:T(8,128)}, f32[24,256]{1,0:T(8,128)}, f32[48,24,128]{2,1,0:T(8,128)}, /*index=5*/f32[48,24,128]{2,1,0:T(8,128)}) custom-call(bf16[48,24,128]{2,1,0:T(8,128)(2,1)} %refs_0_.1, bf16[48,24,128]{2,1,0:T(8,128)(2,1)} %refs_1_.1, ...), custom_call_target="tpu_custom_call" | custom-call | tf_op jit(solution)/shard_map/main/pallas_call | solution.py:619
  94.9 5.0 %finish.1 = (bf16[48,24,128]{2,1,0:T(8,128)(2,1)}, bf16[48,24,128]{2,1,0:T(8,128)(2,1)}, f32[128,512]{1,0:T(8,128)}) custom-call(bf16[16,80,128]{2,1,0:T(8,128)(2,1)} %get-tuple-element.9.land_u, bf16[16,80,128]{2,1,0:T(8,128)(2,1)} %get-tuple-element.10.land_a, f32[128,512]{1,0:T(8,128)} %get-tuple-element.11.proj_in, f32[24,256]{1,0:T(8,128)} %get-tuple-element.12.h_sum, ...), custom_call_target="tpu_custom_call" | custom-call | tf_op jit(solution)/shard_map/finish/pallas_call | solution.py:648
  (1 shorter events, 0.0 us)
Async XLA Ops:
  1.3 0.7 copy-start.1
  1.9 0.7 copy-start

commit v3 on v2

--- a/solution.py
+++ b/solution.py
@@ -23,7 +23,7 @@
 SLOT = 64
 PAIR = 2 * SLOT
 SCALE = DH ** (-0.5)
-VMEM_LIMIT = 60 * 1024 * 1024
+VMEM_LIMIT = 48 * 1024 * 1024
 NT = (((1,), (1,)), ((), ()))
 
 
@@ -35,10 +35,23 @@
         self.part = lax.rem(self.z, 2)
         self.zz = lax.div(self.z, 2)
         self.stays = self.part == self.e
+        self.y = lax.div(self.c, 4)
+        self.x = lax.rem(self.c, 4)
+        self.f = self.x * (1 - self.e) + self.y * self.e
+        self.g = self.y * (1 - self.e) + self.x * self.e
         self.row0 = (self.zz * 2 + self.e) * TALL + self.c * OWN
 
     def swapped(self, c):
         return (self.part, self.zz * 2 + self.e, c)
+
+    def col(self, f, g):
+        return lax.rem(f, 4) * (1 + 3 * self.e) + lax.rem(g, 4) * (4 - 3 * self.e)
+
+    def fpeer(self, n):
+        return (self.e, self.z, self.col(self.f + n, self.g))
+
+    def gpeer(self, n):
+        return (self.e, self.z, self.col(self.f, self.g + n))
 
     def plane(self, n):
         return (self.e, self.z, lax.rem(self.c + n, COLS))
@@ -149,8 +162,8 @@
     lax.fori_loop(0, COLS, column, 0)
 
 
-def repeat_heads(w_bias):
-    wide = w_bias[...].astype(F32)
+def repeat_heads(w_bias_t):
+    wide = jnp.concatenate([w_bias_t[...].astype(F32), jnp.zeros((C - H, C), F32)], axis=0).T
     lane = lax.div(lax.broadcasted_iota(jnp.int32, (C, H * SLOT), 1), SLOT)
     total = jnp.zeros((C, H * SLOT), F32)
     for h in range(H):
@@ -177,9 +190,10 @@
 
 MAIN_SCRATCH = dict(
     m1=((COLS, PADDED, C), BF16),
-    m2=((COLS, PART + WIDTH, C), BF16),
+    m2=((COLS, PADDED, C), BF16),
     in1=((COLS, PADDED, C), BF16),
-    in2=((COLS, PART + WIDTH, C), BF16),
+    in2=((COLS, PADDED, C), BF16),
+    flags=((WIDTH, C), F32),
     w_proj_t=((3 * HD, C), BF16),
     w_rep=((C, H * SLOT), BF16),
     home_rows=((TALL, WIDTH, C), F32),
@@ -188,10 +202,15 @@
     bias=((H, COLS, WIDTH, N), F32),
     d_bias=((H, COLS, WIDTH, N), F32),
     d_other=((2, COLS, WIDTH, N), F32),
-    d_plane=((2, COLS, WIDTH, N), F32),
+    stage_far=((4, WIDTH, N), F32),
+    d_far=((2, 3, 4 * WIDTH, N), BF16),
+    d_far_in=((2, 3, 4 * WIDTH, N), BF16),
+    d_near=((2, 4, WIDTH, N), F32),
+    d_near_in=((2, 3, WIDTH, N), F32),
     zout=((ROWS, WIDTH, PAIR), F32),
     hin=((2, 4, WIDTH, PAIR), F32),
-    mask=((N, C), F32),
+    mask=((COLS, WIDTH, C), F32),
+    row_mask=((OWN, 1, C), F32),
     normed=((OWN, N, C), BF16),
     unit=((OWN, N, C), F32),
     rstd=((OWN, N, C), F32),
@@ -206,6 +225,8 @@
     gate=((OWN, N, C), F32),
     dgate=((OWN, N, C), F32),
     att_t=((OWN, HD, N), F32),
+    att=((OWN, N, HD), F32),
+    d_proj=((OWN, N, 4 * HD), BF16),
     dq_t=((OWN, HD, N), F32),
     dk=((OWN, N, HD), F32),
     dv=((OWN, N, HD), F32),
@@ -223,10 +244,12 @@
     in1=(COLS,),
     in2=(COLS,),
     z=(8,),
-    plane=(2, COLS),
+    near=(2, 3),
+    far=(2, 4, 3),
     partner=(2,),
     back=(2,),
-    d_plane=(2, COLS),
+    d_far=(2, 3),
+    d_near=(2, 3),
     dz=(8,),
     p1=(COLS,),
     p2=(8,),
@@ -234,7 +257,7 @@
     u=(COLS,),
     a=(COLS,),
 )
-MAIN_IN = 9
+MAIN_IN = 10
 MAIN_OUT = 6
 
 
@@ -243,7 +266,7 @@
 
 
 def main_kernel(*refs):
-    (pair, cot, flags, gain, shift, w_proj, gate_bias, w_bias, w_out) = refs[:MAIN_IN]
+    (pair, cot, residues, length, gain, shift, w_proj, gate_bias, w_bias_t, w_out) = refs[:MAIN_IN]
     (land_u, land_a, proj_out, h_sum, home_unit, home_rstd) = refs[MAIN_IN : MAIN_IN + MAIN_OUT]
     rest = refs[MAIN_IN + MAIN_OUT :]
     m, send, recv = Names(), Names(), Names()
@@ -258,21 +281,26 @@
     e = at.e
     count = greet_all(at)
 
+    sublane = lax.broadcasted_iota(jnp.int32, (WIDTH, WIDTH), 0)
+    lane = lax.broadcasted_iota(jnp.int32, (WIDTH, WIDTH), 1)
+    valid = jnp.where(lane + at.c * WIDTH < length[0], residues[...], 0).astype(F32)
+    valid = jnp.sum(jnp.where(lane == sublane, valid, 0.0), axis=1, keepdims=True)
+    m.flags[...] = jnp.broadcast_to(valid, (WIDTH, C))
+    lane = lax.broadcasted_iota(jnp.int32, (8, C), 1)
+    packed_flags = jnp.where(
+        lane == 0, m.flags[0:8, :], jnp.where(lane == 1, m.flags[8:16, :], m.flags[16:24, :])
+    )
+    pad = jnp.zeros((COLS, PADDED - PART, C), F32)
     m.m1[...] = jnp.concatenate(
-        [pair[...].astype(F32).reshape(COLS, PART, C), jnp.zeros((COLS, PADDED - PART, C), F32)], axis=1
-    ).astype(BF16)
-    m.m2[...] = jnp.concatenate(
         [
-            cot[...].astype(F32).reshape(COLS, PART, C),
-            jnp.broadcast_to(flags[...][None], (COLS, WIDTH, C)),
+            pair[...].astype(F32).reshape(COLS, PART, C),
+            jnp.broadcast_to(packed_flags[None], (COLS, PADDED - PART, C)),
         ],
         axis=1,
     ).astype(BF16)
-    pl.semaphore_wait(pltpu.get_barrier_semaphore(), count)
-    exchange_start(at, m.m1, m.in1, send.in1, recv.in1)
-    exchange_start(at, m.m2, m.in2, send.in2, recv.in2)
-
-    m.w_rep[...] = repeat_heads(w_bias)
+    m.m2[...] = jnp.concatenate([cot[...].astype(F32).reshape(COLS, PART, C), pad], axis=1).astype(BF16)
+
+    m.w_rep[...] = repeat_heads(w_bias_t)
     unit, inverse = standardize(pair[...].astype(F32).reshape(TALL * WIDTH, C))
     home_unit[...] = unit.reshape(TALL, WIDTH, C)
     home_rstd[...] = inverse.reshape(TALL, WIDTH, C)
@@ -285,9 +313,11 @@
         return total
 
     packed = lax.fori_loop(0, TALL // 8, home_bias, jnp.zeros((WIDTH, H * SLOT), F32))
-    negative = (flags[...] - 1.0) * 1e9
+    negative = (m.flags[...] - 1.0) * 1e9
     m.zpack[0] = packed[:, :PAIR] + negative
     m.zpack[1] = packed[:, PAIR:] + negative
+
+    pl.semaphore_wait(pltpu.get_barrier_semaphore(), count)
 
     def to_workers(n, carry):
         core, zz = lax.div(n, 4), lax.rem(n, 4)
@@ -302,6 +332,8 @@
         return carry
 
     lax.fori_loop(0, 8, to_workers, 0)
+    exchange_start(at, m.m1, m.in1, send.in1, recv.in1)
+    exchange_start(at, m.m2, m.in2, send.in2, recv.in2)
 
     m.w_proj_t[...] = w_proj[:, : 3 * HD].astype(F32).T.astype(BF16)
     m.d_bias[...] = jnp.zeros_like(m.d_bias)
@@ -315,6 +347,19 @@
         m.unit[s] = unit
         m.rstd[s] = inverse
         m.normed[s] = (unit * gain[...] + shift[...]).astype(BF16)
+
+    def bias_block(hh, a, b):
+        return m.bias.at[e * 2 + hh, at.col(at.f - a + 4, at.g - b + 4)]
+
+    def to_far(hh, a):
+        block = bias_block(hh, a, 0)
+        for n in (1, 2, 3):
+            remote(block, block, send.far.at[hh, a, n - 1], recv.far.at[hh, a, n - 1], at.gpeer(n)).start()
+
+    def forward(hh):
+        for n in (1, 2, 3):
+            arrived(bias_block(hh, n, 0), recv.near.at[hh, n - 1])
+            to_far(hh, n)
 
     for z in range(ROWS):
         arrived(m.zin.at[z], recv.z.at[z])
@@ -324,12 +369,9 @@
             [m.zin[z][:, hh * SLOT : hh * SLOT + TALL] for z in range(ROWS)], axis=1
         )
         mine = m.bias.at[head, at.c]
-
-        def to_plane(n, carry):
-            remote(mine, mine, send.plane.at[hh, n], recv.plane.at[hh, n], at.plane(n)).start()
-            return carry
-
-        lax.fori_loop(1, COLS, to_plane, 0)
+        for n in (1, 2, 3):
+            remote(mine, mine, send.near.at[hh, n - 1], recv.near.at[hh, n - 1], at.fpeer(n)).start()
+        to_far(hh, 0)
 
     for s in range(OWN):
         rows = m.normed[s]
@@ -343,11 +385,19 @@
         m.k_t[s] = flat_t[HD : 2 * HD].astype(BF16)
         m.v_t[s] = flat_t[2 * HD : 3 * HD].astype(BF16)
 
+    forward(0)
+    forward(1)
     exchange_arrived(m.in2, recv.in2)
-    m.mask[...] = m.in2[:, PART : PART + WIDTH, :].astype(F32).reshape(N, C)
+    tiles = m.in1[:, PART:, :].astype(F32)
+    for t in range(3):
+        rows = jnp.broadcast_to(tiles[:, :, t : t + 1], (COLS, 8, C))
+        m.mask[:, t * 8 : (t + 1) * 8, :] = rows
     for s in range(OWN):
         values = m.in2[:, s * WIDTH : (s + 1) * WIDTH, :].astype(F32).reshape(N, C)
-        pair_mask = m.mask[...] * m.mask[pl.ds(at.row0 + s, 1), :]
+        row = at.row0 + s
+        own_mask = m.mask[lax.div(row, WIDTH), pl.ds(lax.rem(row, WIDTH), 1), :]
+        m.row_mask[s] = own_mask
+        pair_mask = m.mask[...].reshape(N, C) * own_mask
         d_out = jnp.where(pair_mask > 0, values, 0.0).astype(BF16)
         d_gated = lax.dot_general(d_out, w_out[...], NT, preferred_element_type=F32)
         gates = m.gate[s]
@@ -357,14 +407,10 @@
         m.dgate[s] = d_attn * (1.0 - gates)
 
     def own_bias_arrived(hh):
-        head = e * 2 + hh
-
-        def from_plane(n, carry):
-            arrived(m.bias.at[head, lax.rem(at.c - n + COLS, COLS)], recv.plane.at[hh, n])
-            return carry
-
-        lax.fori_loop(1, COLS, from_plane, 0)
-        whole = m.bias.at[head]
+        for a in range(4):
+            for n in (1, 2, 3):
+                arrived(bias_block(hh, a, n), recv.far.at[hh, a, n - 1])
+        whole = m.bias.at[e * 2 + hh]
         remote(whole, whole, send.partner.at[hh], recv.partner.at[hh], at.partner()).start()
 
     def other_bias_arrived(hh):
@@ -410,29 +456,45 @@
         head = (1 - e) * 2 + hh
         remote(m.d_bias.at[head], m.d_other.at[hh], send.back.at[hh], recv.back.at[hh], at.partner()).start()
 
-    def scatter_plane(hh):
+    def scatter_far(hh):
         head = e * 2 + hh
         arrived(m.d_other.at[hh], recv.back.at[hh])
-        m.d_bias[head] += m.d_other[hh]
-
-        def to_plane(n, carry):
+        for n in (1, 2, 3, 0):
+            for f in range(4):
+                column = at.col(f, at.g + n)
+                both = m.d_bias[head, column] + m.d_other[hh, column]
+                if n == 0:
+                    m.d_near[hh, f] = both
+                else:
+                    m.stage_far[f] = both
+            if n > 0:
+                m.d_far[hh, n - 1] = m.stage_far[...].reshape(4 * WIDTH, N).astype(BF16)
+                remote(
+                    m.d_far.at[hh, n - 1],
+                    m.d_far_in.at[hh, n - 1],
+                    send.d_far.at[hh, n - 1],
+                    recv.d_far.at[hh, n - 1],
+                    at.gpeer(n),
+                ).start()
+
+    def scatter_near(hh):
+        for n in range(3):
+            arrived(m.d_far_in.at[hh, n], recv.d_far.at[hh, n])
+        far = (m.d_far_in[hh, 0].astype(F32) + m.d_far_in[hh, 1].astype(F32)) + m.d_far_in[hh, 2].astype(F32)
+        m.d_near[hh] += far.reshape(4, WIDTH, N)
+        for n in (1, 2, 3):
             remote(
-                m.d_bias.at[head, lax.rem(at.c + n, COLS)],
-                m.d_plane.at[hh, n],
-                send.d_plane.at[hh, n],
-                recv.d_plane.at[hh, n],
-                at.plane(n),
+                m.d_near.at[hh, lax.rem(at.f + n, 4)],
+                m.d_near_in.at[hh, n - 1],
+                send.d_near.at[hh, n - 1],
+                recv.d_near.at[hh, n - 1],
+                at.fpeer(n),
             ).start()
-            return carry
-
-        lax.fori_loop(1, COLS, to_plane, 0)
 
     def plane_sum(hh):
-        def from_plane(n, total):
-            arrived(m.d_plane.at[hh, n], recv.d_plane.at[hh, n])
-            return total + m.d_plane[hh, n]
-
-        return lax.fori_loop(1, COLS, from_plane, m.d_bias[e * 2 + hh, at.c])
+        for n in range(3):
+            arrived(m.d_near_in.at[hh, n], recv.d_near.at[hh, n])
+        return (m.d_near[hh, at.f] + m.d_near_in[hh, 0]) + (m.d_near_in[hh, 1] + m.d_near_in[hh, 2])
 
     own_bias_arrived(0)
     attend(e * 2)
@@ -443,33 +505,24 @@
     other_bias_arrived(1)
     attend(3 - e * 2)
     to_other(1)
-    scatter_plane(0)
+    scatter_far(0)
     attend(e * 2 + 1)
-    scatter_plane(1)
+    scatter_far(1)
+    scatter_near(0)
 
     for s in range(OWN):
         attended = m.att_t[s].T
-        gated = (m.gate[s] * attended).astype(BF16)
-        pair_mask = m.mask[...] * m.mask[pl.ds(at.row0 + s, 1), :]
-        update = jnp.dot(gated, w_out[...], preferred_element_type=F32) * pair_mask
+        m.att[s] = attended
         d_proj = jnp.concatenate(
             [m.dq_t[s].T * SCALE, m.dk[s], m.dv[s], m.dgate[s] * attended], axis=1
         ).astype(BF16)
-        d_normed = lax.dot_general(d_proj, w_proj[...], NT, preferred_element_type=F32)
-        result = norm_backward(d_normed * gain[...], m.unit[s], m.rstd[s])
-        m.stage_u[:, s * WIDTH : (s + 1) * WIDTH, :] = update.reshape(COLS, WIDTH, C)
-        m.stage_a[:, s * WIDTH : (s + 1) * WIDTH, :] = result.reshape(COLS, WIDTH, C)
+        m.d_proj[s] = d_proj
         normed_t = m.normed[s].astype(F32).T.astype(BF16)
         share = jnp.dot(normed_t, d_proj, preferred_element_type=F32)
         if s == 0:
             m.proj[...] = share
         else:
             m.proj[...] += share
-    pad = jnp.zeros((COLS, PADDED - PART, C), F32)
-    m.stage_u[:, PART:, :] = pad
-    m.stage_a[:, PART:, :] = pad
-    m.out_u[...] = m.stage_u[...].astype(BF16)
-    m.out_a[...] = m.stage_a[...].astype(BF16)
 
     def rows_of(ref, c):
         return ref.at[pl.ds(pl.multiple_of(c * 8, 8), 8), :]
@@ -480,8 +533,16 @@
         return carry
 
     lax.fori_loop(1, COLS, scatter_proj, 0)
+    scatter_near(1)
+
+    for s in range(OWN):
+        gated = (m.gate[s] * m.att[s]).astype(BF16)
+        pair_mask = m.mask[...].reshape(N, C) * m.row_mask[s]
+        update = jnp.dot(gated, w_out[...], preferred_element_type=F32) * pair_mask
+        m.stage_u[:, s * WIDTH : (s + 1) * WIDTH, :] = update.reshape(COLS, WIDTH, C)
+    m.stage_u[:, PART:, :] = pad
+    m.out_u[...] = m.stage_u[...].astype(BF16)
     exchange_start(at, m.out_u, land_u, send.u, recv.u)
-    exchange_start(at, m.out_a, land_a, send.a, recv.a)
 
     halves = [plane_sum(0), plane_sum(1)]
     blank = jnp.zeros((WIDTH, SLOT - TALL), F32)
@@ -502,6 +563,14 @@
 
     lax.fori_loop(0, ROWS, to_homes, 0)
 
+    for s in range(OWN):
+        d_normed = lax.dot_general(m.d_proj[s], w_proj[...], NT, preferred_element_type=F32)
+        result = norm_backward(d_normed * gain[...], m.unit[s], m.rstd[s])
+        m.stage_a[:, s * WIDTH : (s + 1) * WIDTH, :] = result.reshape(COLS, WIDTH, C)
+    m.stage_a[:, PART:, :] = pad
+    m.out_a[...] = m.stage_a[...].astype(BF16)
+    exchange_start(at, m.out_a, land_a, send.a, recv.a)
+
     def proj_arrived(n, total):
         arrived(m.r5.at[n], recv.p1.at[n])
         return total + m.r5[n]
@@ -544,9 +613,6 @@
     lax.fori_loop(0, COLS, out_arrived, 0)
 
     def column_sent(n, carry):
-        for hh in range(2):
-            arrived(m.bias.at[0, 0], send.plane.at[hh, n])
-            arrived(m.d_bias.at[0, 0], send.d_plane.at[hh, n])
         arrived(m.v5, send.p1.at[n])
         arrived(m.v6, send.p3.at[n])
         return carry
@@ -567,6 +633,12 @@
 
     lax.fori_loop(0, 8, column_group_sent, 0)
     for hh in range(2):
+        for n in range(3):
+            arrived(m.bias.at[0, 0], send.near.at[hh, n])
+            for a in range(4):
+                arrived(m.bias.at[0, 0], send.far.at[hh, a, n])
+            arrived(m.d_far.at[0, 0], send.d_far.at[hh, n])
+            arrived(m.d_near.at[0, 0], send.d_near.at[hh, n])
         arrived(m.bias.at[0], send.partner.at[hh])
         arrived(m.d_bias.at[0], send.back.at[hh])
     exchange_sent(at, m.m1, send.in1)
@@ -576,12 +648,12 @@
 
 
 def finish_kernel(
-    land_u, land_a, proj_in, h_sum, unit, rstd, gain, w_bias, update, pair_grad, proj_out, w_rep, split, share
+    land_u, land_a, proj_in, h_sum, unit, rstd, gain, w_bias_t, update, pair_grad, proj_out, w_rep, split, share
 ):
     proj_out[...] = proj_in[...]
     update[...] = land_u[:, :PART, :].astype(F32).reshape(TALL, WIDTH, C).astype(BF16)
     share[...] = land_a[:, :PART, :].astype(F32).reshape(TALL, WIDTH, C)
-    w_rep[...] = repeat_heads(w_bias)
+    w_rep[...] = repeat_heads(w_bias_t)
     total = h_sum[...]
     for n in range(3):
         term = total.astype(BF16).astype(F32)
@@ -609,8 +681,6 @@
     pair_act, cotangent, ln_gain, ln_shift, w_proj, gate_bias, w_bias, w_out, residue_mask, valid_length
 ):
     any_space = pl.BlockSpec(memory_space=pl.ANY)
-    positions = lax.axis_index("col") * WIDTH + lax.iota(jnp.int32, WIDTH)
-    flags = jnp.where(positions < valid_length[0], residue_mask, 0).astype(F32)
     gain = ln_gain.reshape(1, C)
     sems = [pltpu.SemaphoreType.DMA(shape) for shape in MAIN_SEMS.values()]
     landing = jax.ShapeDtypeStruct((COLS, PADDED, C), BF16)
@@ -626,7 +696,7 @@
             block,
             block,
         ],
-        in_specs=vmem(MAIN_IN),
+        in_specs=vmem(3) + [pl.BlockSpec(memory_space=pltpu.SMEM)] + vmem(MAIN_IN - 4),
         out_specs=[any_space] * 3 + vmem(3),
         scratch_shapes=[pltpu.VMEM(shape, dtype) for shape, dtype in MAIN_SCRATCH.values()] + sems + sems,
         compiler_params=pltpu.CompilerParams(
@@ -636,12 +706,13 @@
     )(
         pair_act,
         cotangent,
-        jnp.broadcast_to(flags[:, None], (WIDTH, C)),
+        residue_mask.reshape(1, WIDTH),
+        valid_length,
         gain,
         ln_shift.reshape(1, C),
         w_proj,
         gate_bias.reshape(1, HD),
-        w_bias,
+        w_bias.T,
         w_out,
     )
     result = jax.ShapeDtypeStruct(pair_act.shape, BF16)
@@ -657,7 +728,7 @@
         ],
         compiler_params=pltpu.CompilerParams(vmem_limit_bytes=VMEM_LIMIT),
         name="finish",
-    )(land_u, land_a, proj, h_sum, unit, rstd, gain, w_bias)
+    )(land_u, land_a, proj, h_sum, unit, rstd, gain, w_bias.T)
 
 
 def solution(mesh):

time: 100 us -> 92.7 us (0.927)
  Pallas kernels: 96.5 us -> 86.4 us
  local copies, waits for them, and re-layouts: 2.06 us -> 4.27 us
    pallas_call x1, Pallas kernels: 91.5 us -> 82.9 us  [shards(): pl.pallas_call(main_kernel, out_shape=[landing, landing, proj_shape, jax....]
    unnamed x5 -> x18, local copies, waits for them, and re-layouts: 1.39 us -> 4.27 us
    pallas_call x1, Pallas kernels: 4.98 us -> 3.47 us  [shards(): pl.pallas_call(finish_kernel, out_shape=[result, result, proj_shape], in_...]
where the time goes in v3:
time: 92.7 us; the launch traced here: 92 us
  Pallas kernels  86.4 us (93%)
  local copies, waits for them, and re-layouts  4.27 us (5%)
  between operations  1.34 us (1%)
    pallas_call x1, Pallas kernels, shards(): pl.pallas_call(main_kernel, out_shape=[landing, landing, proj_shape, jax....  82.9 us
    unnamed x18, local copies, waits for them, and re-layouts  4.27 us
    pallas_call x1, Pallas kernels, shards(): pl.pallas_call(finish_kernel, out_shape=[result, result, proj_shape], in_...  3.47 us

profile of v3, /device:TPU:1, one launch (start us, length us, event | category | flops | bytes accessed | tf_op | source)
XLA Modules:
  0.0 92.0 jit_solution(7348479133946593088)
XLA Ops:
  1.3 0.0 copy-start.6
  1.3 0.0 copy-start.7
  1.3 0.0 copy-start.8
  1.3 0.0 copy-start.4
  1.3 0.0 copy-start.5
  1.3 0.6 copy-done.6
  1.9 0.0 copy-done.7
  2.0 0.0 copy-done.8
  2.0 0.0 copy-done.4
  2.0 0.0 copy-done.5
  2.0 0.0 copy-start
  2.0 1.0 %copy-done = bf16[48,24,128]{2,1,0:T(8,128)(2,1)S(1)} copy-done((bf16[48,24,128]{2,1,0:T(8,128)(2,1)S(1)}, bf16[48,24,128]{2,1,0:T(8,128)(2,1)}, u32[]{:S(2)}) %copy-start) | copy-done | bytes 294936
  3.0 0.0 copy-start.1
  3.0 1.0 %copy-done.1 = bf16[48,24,128]{2,1,0:T(8,128)(2,1)S(1)} copy-done((bf16[48,24,128]{2,1,0:T(8,128)(2,1)S(1)}, bf16[48,24,128]{2,1,0:T(8,128)(2,1)}, u32[]{:S(2)}) %copy-start.1) | copy-done | bytes 294936
  3.9 0.0 copy-start.2
  3.9 0.9 copy-done.2
  4.8 0.0 copy-start.3
  4.8 0.8 copy-done.3
  5.6 82.9 %main.1 = (bf16[16,80,128]{2,1,0:T(8,128)(2,1)S(1)}, bf16[16,80,128]{2,1,0:T(8,128)(2,1)S(1)}, f32[128,512]{1,0:T(8,128)S(1)}, f32[24,256]{1,0:T(8,128)S(1)}, f3...) custom-call(bf16[48,24,128]{2,1,0:T(8,128)(2,1)S(1)} %copy-done, bf16[48,24,128]{2,1,0:T(8,128)(2,1)S(1)} %copy-done.1, ...), custom_call_target="tpu_custom_call" | custom-call | tf_op jit(solution)/shard_map/main/pallas_call | solution.py:689
  88.5 3.5 %finish.1 = (bf16[48,24,128]{2,1,0:T(8,128)(2,1)}, bf16[48,24,128]{2,1,0:T(8,128)(2,1)}, f32[128,512]{1,0:T(8,128)}) custom-call(bf16[16,80,128]{2,1,0:T(8,128)(2,1)S(1)} %get-tuple-element.9.land_u, bf16[16,80,128]{2,1,0:T(8,128)(2,1)S(1)} %get-tuple-element.10.land_a, f32[128,512]{1,0:T(8,128)S(1)} %get-tuple-element.11.proj_in, ...), custom_call_target="tpu_custom_call" | custom-call | tf_op jit(solution)/shard_map/finish/pallas_call | solution.py:719
Async XLA Ops:
  1.3 0.7 copy-start.6
  1.3 0.7 copy-start.7
  1.3 0.7 copy-start.8
  1.3 0.7 copy-start.4
  1.3 0.7 copy-start.5
  2.0 1.0 %copy-start = (bf16[48,24,128]{2,1,0:T(8,128)(2,1)S(1)}, bf16[48,24,128]{2,1,0:T(8,128)(2,1)}, u32[]{:S(2)}) copy-start(bf16[48,24,128]{2,1,0:T(8,128)(2,1)} %refs_0_.1) | copy-start | bytes 884740
  3.0 1.0 %copy-start.1 = (bf16[48,24,128]{2,1,0:T(8,128)(2,1)S(1)}, bf16[48,24,128]{2,1,0:T(8,128)(2,1)}, u32[]{:S(2)}) copy-start(bf16[48,24,128]{2,1,0:T(8,128)(2,1)} %refs_1_.1) | copy-start | bytes 884740
  3.9 0.9 copy-start.2
  4.8 0.8 copy-start.3

commit v4 on v3

--- a/solution.py
+++ b/solution.py
@@ -23,7 +23,7 @@
 SLOT = 64
 PAIR = 2 * SLOT
 SCALE = DH ** (-0.5)
-VMEM_LIMIT = 48 * 1024 * 1024
+VMEM_LIMIT = 60 * 1024 * 1024
 NT = (((1,), (1,)), ((), ()))
 
 
@@ -189,6 +189,19 @@
 
 
 MAIN_SCRATCH = dict(
+    pair=((TALL, WIDTH, C), BF16),
+    cot=((TALL, WIDTH, C), BF16),
+    residues=((1, WIDTH), jnp.int32),
+    gain=((1, C), F32),
+    shift=((1, C), F32),
+    w_proj=((C, 4 * HD), BF16),
+    gate_bias=((1, HD), F32),
+    w_bias_t=((H, C), BF16),
+    w_out=((HD, C), BF16),
+    home_unit=((TALL, WIDTH, C), F32),
+    home_rstd=((TALL, WIDTH, C), F32),
+    scores=((H, OWN, N, N), F32),
+    d_prob=((H, OWN, N, N), F32),
     m1=((COLS, PADDED, C), BF16),
     m2=((COLS, PADDED, C), BF16),
     in1=((COLS, PADDED, C), BF16),
@@ -241,6 +254,8 @@
     out_a=((COLS, PADDED, C), BF16),
 )
 MAIN_SEMS = dict(
+    operand=(9,),
+    norm=(2,),
     in1=(COLS,),
     in2=(COLS,),
     z=(8,),
@@ -266,8 +281,8 @@
 
 
 def main_kernel(*refs):
-    (pair, cot, residues, length, gain, shift, w_proj, gate_bias, w_bias_t, w_out) = refs[:MAIN_IN]
-    (land_u, land_a, proj_out, h_sum, home_unit, home_rstd) = refs[MAIN_IN : MAIN_IN + MAIN_OUT]
+    length, operands = refs[0], refs[1:MAIN_IN]
+    (land_u, land_a, proj_out, h_sum, unit_out, rstd_out) = refs[MAIN_IN : MAIN_IN + MAIN_OUT]
     rest = refs[MAIN_IN + MAIN_OUT :]
     m, send, recv = Names(), Names(), Names()
     for name, ref in zip(MAIN_SCRATCH, rest):
@@ -277,9 +292,15 @@
         setattr(send, name, ref)
     for name, ref in zip(MAIN_SEMS, rest[len(MAIN_SEMS) :]):
         setattr(recv, name, ref)
+    held = (m.pair, m.cot, m.residues, m.gain, m.shift, m.w_proj, m.gate_bias, m.w_bias_t, m.w_out)
+    pair, cot, residues, gain, shift, w_proj, gate_bias, w_bias_t, w_out = held
+    for n in range(MAIN_IN - 1):
+        pltpu.make_async_copy(operands[n], held[n], recv.operand.at[n]).start()
     at = Place()
     e = at.e
     count = greet_all(at)
+    for n in range(MAIN_IN - 1):
+        arrived(held[n], recv.operand.at[n])
 
     sublane = lax.broadcasted_iota(jnp.int32, (WIDTH, WIDTH), 0)
     lane = lax.broadcasted_iota(jnp.int32, (WIDTH, WIDTH), 1)
@@ -302,8 +323,8 @@
 
     m.w_rep[...] = repeat_heads(w_bias_t)
     unit, inverse = standardize(pair[...].astype(F32).reshape(TALL * WIDTH, C))
-    home_unit[...] = unit.reshape(TALL, WIDTH, C)
-    home_rstd[...] = inverse.reshape(TALL, WIDTH, C)
+    m.home_unit[...] = unit.reshape(TALL, WIDTH, C)
+    m.home_rstd[...] = inverse.reshape(TALL, WIDTH, C)
     m.home_rows[...] = (unit * gain[...] + shift[...]).reshape(TALL, WIDTH, C)
 
     def home_bias(n, total):
@@ -334,6 +355,8 @@
     lax.fori_loop(0, 8, to_workers, 0)
     exchange_start(at, m.m1, m.in1, send.in1, recv.in1)
     exchange_start(at, m.m2, m.in2, send.in2, recv.in2)
+    pltpu.make_async_copy(m.home_unit, unit_out, recv.norm.at[0]).start()
+    pltpu.make_async_copy(m.home_rstd, rstd_out, recv.norm.at[1]).start()
 
     m.w_proj_t[...] = w_proj[:, : 3 * HD].astype(F32).T.astype(BF16)
     m.d_bias[...] = jnp.zeros_like(m.d_bias)
@@ -406,6 +429,16 @@
         m.d_t[s] = d_attn.T.astype(BF16)
         m.dgate[s] = d_attn * (1.0 - gates)
 
+    def products(h, carry):
+        row = lax.div(lax.broadcasted_iota(jnp.int32, (C, N), 0), DH)
+        by_row = (row == h).astype(F32).astype(BF16)
+        for s in range(OWN):
+            m.scores[h, s] = jnp.dot(m.k[s], m.q_t[s] * by_row, preferred_element_type=F32)
+            m.d_prob[h, s] = jnp.dot(m.v[s], m.d_t[s] * by_row, preferred_element_type=F32)
+        return carry
+
+    lax.fori_loop(0, H, products, 0)
+
     def own_bias_arrived(hh):
         for a in range(4):
             for n in (1, 2, 3):
@@ -419,26 +452,21 @@
     def attend(h):
         here = pl.ds(pl.multiple_of(h * DH, DH), DH)
         lane = lax.div(lax.broadcasted_iota(jnp.int32, (C, C), 1), DH)
-        row = lax.div(lax.broadcasted_iota(jnp.int32, (C, C), 0), DH)
         by_lane = (lane == h).astype(F32).astype(BF16)
-        by_row = (row == h).astype(F32).astype(BF16)
 
         def one_row(s, carry):
-            keys, values = m.k[s], m.v[s]
             keys_t, values_t = m.k_t[s, here, :], m.v_t[s, here, :]
             dk_sum = dv_sum = None
             for n in range(3):
                 lanes = slice(n * C, (n + 1) * C)
-                scores = jnp.dot(keys, m.q_t[s, :, lanes] * by_row, preferred_element_type=F32)
-                scores = scores + m.bias[h, :, :, lanes].reshape(N, C)
+                scores = m.scores[h, s, :, lanes] + m.bias[h, :, :, lanes].reshape(N, C)
                 exponent = jnp.exp(scores - jnp.max(scores, axis=0, keepdims=True))
                 weights = exponent * (1.0 / jnp.sum(exponent, axis=0, keepdims=True))
                 weights_b = weights.astype(BF16)
                 attended = jnp.dot(values_t, weights_b, preferred_element_type=F32)
                 m.att_t[s, here, lanes] = attended
                 delta = jnp.sum(attended * m.d_t[s, here, lanes].astype(F32), axis=0, keepdims=True)
-                d_prob = jnp.dot(values, m.d_t[s, :, lanes] * by_row, preferred_element_type=F32)
-                d_score = weights * (d_prob - delta)
+                d_score = weights * (m.d_prob[h, s, :, lanes] - delta)
                 d_score_b = d_score.astype(BF16)
                 m.d_bias[h, :, :, lanes] += d_score.reshape(COLS, WIDTH, C)
                 m.dq_t[s, here, lanes] = jnp.dot(keys_t, d_score_b, preferred_element_type=F32)
@@ -508,7 +536,6 @@
     scatter_far(0)
     attend(e * 2 + 1)
     scatter_far(1)
-    scatter_near(0)
 
     for s in range(OWN):
         attended = m.att_t[s].T
@@ -533,7 +560,7 @@
         return carry
 
     lax.fori_loop(1, COLS, scatter_proj, 0)
-    scatter_near(1)
+    scatter_near(0)
 
     for s in range(OWN):
         gated = (m.gate[s] * m.att[s]).astype(BF16)
@@ -543,6 +570,15 @@
     m.stage_u[:, PART:, :] = pad
     m.out_u[...] = m.stage_u[...].astype(BF16)
     exchange_start(at, m.out_u, land_u, send.u, recv.u)
+    scatter_near(1)
+
+    for s in range(OWN):
+        d_normed = lax.dot_general(m.d_proj[s], w_proj[...], NT, preferred_element_type=F32)
+        result = norm_backward(d_normed * gain[...], m.unit[s], m.rstd[s])
+        m.stage_a[:, s * WIDTH : (s + 1) * WIDTH, :] = result.reshape(COLS, WIDTH, C)
+    m.stage_a[:, PART:, :] = pad
+    m.out_a[...] = m.stage_a[...].astype(BF16)
+    exchange_start(at, m.out_a, land_a, send.a, recv.a)
 
     halves = [plane_sum(0), plane_sum(1)]
     blank = jnp.zeros((WIDTH, SLOT - TALL), F32)
@@ -563,13 +599,6 @@
 
     lax.fori_loop(0, ROWS, to_homes, 0)
 
-    for s in range(OWN):
-        d_normed = lax.dot_general(m.d_proj[s], w_proj[...], NT, preferred_element_type=F32)
-        result = norm_backward(d_normed * gain[...], m.unit[s], m.rstd[s])
-        m.stage_a[:, s * WIDTH : (s + 1) * WIDTH, :] = result.reshape(COLS, WIDTH, C)
-    m.stage_a[:, PART:, :] = pad
-    m.out_a[...] = m.stage_a[...].astype(BF16)
-    exchange_start(at, m.out_a, land_a, send.a, recv.a)
 
     def proj_arrived(n, total):
         arrived(m.r5.at[n], recv.p1.at[n])
@@ -611,6 +640,9 @@
         return carry
 
     lax.fori_loop(0, COLS, out_arrived, 0)
+
+    arrived(unit_out, recv.norm.at[0])
+    arrived(rstd_out, recv.norm.at[1])
 
     def column_sent(n, carry):
         arrived(m.v5, send.p1.at[n])
@@ -647,30 +679,35 @@
     exchange_sent(at, m.out_a, send.a)
 
 
+STEPS = 4
+
+
 def finish_kernel(
     land_u, land_a, proj_in, h_sum, unit, rstd, gain, w_bias_t, update, pair_grad, proj_out, w_rep, split, share
 ):
-    proj_out[...] = proj_in[...]
-    update[...] = land_u[:, :PART, :].astype(F32).reshape(TALL, WIDTH, C).astype(BF16)
-    share[...] = land_a[:, :PART, :].astype(F32).reshape(TALL, WIDTH, C)
-    w_rep[...] = repeat_heads(w_bias_t)
-    total = h_sum[...]
-    for n in range(3):
-        term = total.astype(BF16).astype(F32)
-        split[n * WIDTH : (n + 1) * WIDTH, :] = term
-        total = total - term
-
-    def rows(n, carry):
-        terms = split[...].astype(BF16)
-        for inner in range(8):
-            i = n * 8 + inner
-            parts = lax.dot_general(terms, only_row(w_rep[...], i), NT, preferred_element_type=F32)
-            grad = (parts[2 * WIDTH :] + parts[WIDTH : 2 * WIDTH]) + parts[:WIDTH]
-            result = norm_backward(grad * gain[...], unit[i], rstd[i])
-            pair_grad[i] = (share[i] + result).astype(BF16)
-        return carry
-
-    lax.fori_loop(0, TALL // 8, rows, 0)
+    tall = TALL // STEPS
+    step = pl.program_id(0)
+
+    @pl.when(step == 0)
+    def _():
+        proj_out[...] = proj_in[...]
+        w_rep[...] = repeat_heads(w_bias_t)
+        total = h_sum[...]
+        for n in range(3):
+            term = total.astype(BF16).astype(F32)
+            split[n * WIDTH : (n + 1) * WIDTH, :] = term
+            total = total - term
+
+    update[...] = land_u[:, :PART, :].astype(F32).reshape(tall, WIDTH, C).astype(BF16)
+    share[...] = land_a[:, :PART, :].astype(F32).reshape(tall, WIDTH, C)
+    terms = split[...].astype(BF16)
+    for i in range(tall):
+        parts = lax.dot_general(
+            terms, only_row(w_rep[...], step * tall + i), NT, preferred_element_type=F32
+        )
+        grad = (parts[2 * WIDTH :] + parts[WIDTH : 2 * WIDTH]) + parts[:WIDTH]
+        result = norm_backward(grad * gain[...], unit[i], rstd[i])
+        pair_grad[i] = (share[i] + result).astype(BF16)
 
 
 def vmem(count):
@@ -696,18 +733,18 @@
             block,
             block,
         ],
-        in_specs=vmem(3) + [pl.BlockSpec(memory_space=pltpu.SMEM)] + vmem(MAIN_IN - 4),
-        out_specs=[any_space] * 3 + vmem(3),
+        in_specs=[pl.BlockSpec(memory_space=pltpu.SMEM)] + [any_space] * (MAIN_IN - 1),
+        out_specs=[any_space] * 3 + vmem(1) + [any_space] * 2,
         scratch_shapes=[pltpu.VMEM(shape, dtype) for shape, dtype in MAIN_SCRATCH.values()] + sems + sems,
         compiler_params=pltpu.CompilerParams(
             collective_id=0, has_side_effects=True, vmem_limit_bytes=VMEM_LIMIT
         ),
         name="main",
     )(
+        valid_length,
         pair_act,
         cotangent,
         residue_mask.reshape(1, WIDTH),
-        valid_length,
         gain,
         ln_shift.reshape(1, C),
         w_proj,
@@ -716,15 +753,32 @@
         w_out,
     )
     result = jax.ShapeDtypeStruct(pair_act.shape, BF16)
+    tall = TALL // STEPS
+    rows = pl.BlockSpec((tall, WIDTH, C), lambda n: (n, 0, 0))
+    landed = pl.BlockSpec((COLS // STEPS, PADDED, C), lambda n: (n, 0, 0))
+
+    def whole(*shape):
+        return pl.BlockSpec(shape, lambda n: (0,) * len(shape))
+
     return pl.pallas_call(
         finish_kernel,
         out_shape=[result, result, proj_shape],
-        in_specs=vmem(8),
-        out_specs=vmem(3),
+        grid=(STEPS,),
+        in_specs=[
+            landed,
+            landed,
+            whole(C, 4 * HD),
+            whole(WIDTH, H * SLOT),
+            rows,
+            rows,
+            whole(1, C),
+            whole(H, C),
+        ],
+        out_specs=[rows, rows, whole(C, 4 * HD)],
         scratch_shapes=[
             pltpu.VMEM((C, H * SLOT), BF16),
             pltpu.VMEM((3 * WIDTH, H * SLOT), F32),
-            pltpu.VMEM(pair_act.shape, F32),
+            pltpu.VMEM((tall, WIDTH, C), F32),
         ],
         compiler_params=pltpu.CompilerParams(vmem_limit_bytes=VMEM_LIMIT),
         name="finish",

time: 92.7 us -> 82.7 us (0.89)
  Pallas kernels: 86.4 us -> 81.3 us
  local copies, waits for them, and re-layouts: 4.27 us -> 0 us
    pallas_call x1, Pallas kernels: 82.9 us -> 76.4 us  [shards(): pl.pallas_call(main_kernel, out_shape=[landing, landing, proj_shape, jax....]
    unnamed x18 -> x0, local copies, waits for them, and re-layouts: 4.27 us -> none
    pallas_call x1, Pallas kernels: 3.47 us -> 4.89 us  [shards(): pl.pallas_call(finish_kernel, out_shape=[result, result, proj_shape], gri...]
where the time goes in v4:
time: 82.7 us; the launch traced here: 82.6 us
  Pallas kernels  81.3 us (98%)
  between operations  1.29 us (2%)
    pallas_call x1, Pallas kernels, shards(): pl.pallas_call(main_kernel, out_shape=[landing, landing, proj_shape, jax....  76.4 us
    pallas_call x1, Pallas kernels, shards(): pl.pallas_call(finish_kernel, out_shape=[result, result, proj_shape], gri...  4.89 us

profile of v4, /device:TPU:1, one launch (start us, length us, event | category | flops | bytes accessed | tf_op | source)
XLA Modules:
  0.0 82.6 jit_solution(17718973927894244943)
XLA Ops:
  1.3 76.4 %main.1 = (bf16[16,80,128]{2,1,0:T(8,128)(2,1)}, bf16[16,80,128]{2,1,0:T(8,128)(2,1)}, f32[128,512]{1,0:T(8,128)}, f32[24,256]{1,0:T(8,128)}, f32[48,24,128]{2,1,0:T(8,128)}, /*index=5*/f32[48,24,128]{2,1,0:T(8,128)}) custom-call(s32[1]{0:T(128)S(6)} %copy.13.refs_0_, bf16[48,24,128]{2,1,0:T(8,128)(2,1)} %refs_1_.1, bf16[48,24,128]{2,1,0:T(8,128)(2,1)} %refs_2_.1, ...), custom_call_target="tpu_custom_call" | custom-call | tf_op jit(solution)/shard_map/main/pallas_call | solution.py:726
  77.7 4.9 %finish.1 = (bf16[48,24,128]{2,1,0:T(8,128)(2,1)}, bf16[48,24,128]{2,1,0:T(8,128)(2,1)}, f32[128,512]{1,0:T(8,128)}) custom-call(bf16[16,80,128]{2,1,0:T(8,128)(2,1)} %get-tuple-element.9.land_u, bf16[16,80,128]{2,1,0:T(8,128)(2,1)} %get-tuple-element.10.land_a, f32[128,512]{1,0:T(8,128)} %get-tuple-element.11.proj_in, f32[24,256]{1,0:T(8,128)} %get-tuple-element.12.h_sum, ...), custom_call_target="tpu_custom_call" | custom-call | tf_op jit(solution)/shard_map/finish/pallas_call | solution.py:763

commit v5 on v4

--- a/solution.py
+++ b/solution.py
@@ -131,11 +131,11 @@
     return jnp.where(at.stays, COLS - 1 + 7 + 4, COLS - 1 + 8 + 4 + COLS)
 
 
-def exchange_start(at, source, landing, send, recv):
+def exchange_start(at, source, slot, send, recv):
     def column(n, carry):
         t = lax.rem(at.c + n, COLS)
         here = jnp.logical_and(n == 0, at.stays)
-        send_or_copy(here, source.at[t], landing.at[at.c], send.at[t], recv.at[at.c], at.swapped(t))
+        send_or_copy(here, source.at[t], slot, send.at[t], recv.at[at.c], at.swapped(t))
         return carry
 
     lax.fori_loop(0, COLS, column, 0)
@@ -172,7 +172,7 @@
 
 
 def only_row(repeated, i):
-    lane = lax.rem(lax.broadcasted_iota(jnp.int32, (C, H * SLOT), 1), SLOT)
+    lane = lax.rem(lax.broadcasted_iota(jnp.int32, (1, H * SLOT), 1), SLOT)
     return repeated * (lane == i).astype(F32).astype(BF16)
 
 
@@ -238,20 +238,17 @@
     gate=((OWN, N, C), F32),
     dgate=((OWN, N, C), F32),
     att_t=((OWN, HD, N), F32),
-    att=((OWN, N, HD), F32),
-    d_proj=((OWN, N, 4 * HD), BF16),
+
     dq_t=((OWN, HD, N), F32),
     dk=((OWN, N, HD), F32),
     dv=((OWN, N, HD), F32),
     proj=((C, 4 * HD), F32),
-    r5=((COLS, 8, 4 * HD), F32),
-    v5=((8, 4 * HD), F32),
-    r6=((8, 8, 4 * HD), F32),
-    v6=((8, 4 * HD), F32),
-    stage_u=((COLS, PADDED, C), F32),
-    stage_a=((COLS, PADDED, C), F32),
-    out_u=((COLS, PADDED, C), BF16),
-    out_a=((COLS, PADDED, C), BF16),
+    proj_b=((C, 4 * HD), BF16),
+    r5=((COLS, 16, 2 * HD), BF16),
+    v5=((16, 2 * HD), F32),
+    r6=((8, 16, 2 * HD), F32),
+    v6=((16, 2 * HD), BF16),
+    out=((OWN, COLS, 2 * WIDTH, C), BF16),
 )
 MAIN_SEMS = dict(
     operand=(9,),
@@ -269,11 +266,10 @@
     p1=(COLS,),
     p2=(8,),
     p3=(COLS,),
-    u=(COLS,),
-    a=(COLS,),
+    out=(OWN, COLS),
 )
 MAIN_IN = 10
-MAIN_OUT = 6
+MAIN_OUT = 5
 
 
 class Names:
@@ -282,7 +278,7 @@
 
 def main_kernel(*refs):
     length, operands = refs[0], refs[1:MAIN_IN]
-    (land_u, land_a, proj_out, h_sum, unit_out, rstd_out) = refs[MAIN_IN : MAIN_IN + MAIN_OUT]
+    (land, proj_out, h_sum, unit_out, rstd_out) = refs[MAIN_IN : MAIN_IN + MAIN_OUT]
     rest = refs[MAIN_IN + MAIN_OUT :]
     m, send, recv = Names(), Names(), Names()
     for name, ref in zip(MAIN_SCRATCH, rest):
@@ -353,8 +349,8 @@
         return carry
 
     lax.fori_loop(0, 8, to_workers, 0)
-    exchange_start(at, m.m1, m.in1, send.in1, recv.in1)
-    exchange_start(at, m.m2, m.in2, send.in2, recv.in2)
+    exchange_start(at, m.m1, m.in1.at[at.c], send.in1, recv.in1)
+    exchange_start(at, m.m2, m.in2.at[at.c], send.in2, recv.in2)
     pltpu.make_async_copy(m.home_unit, unit_out, recv.norm.at[0]).start()
     pltpu.make_async_copy(m.home_rstd, rstd_out, recv.norm.at[1]).start()
 
@@ -362,6 +358,7 @@
     m.d_bias[...] = jnp.zeros_like(m.d_bias)
     m.dk[...] = jnp.zeros_like(m.dk)
     m.dv[...] = jnp.zeros_like(m.dv)
+    m.proj[...] = jnp.zeros_like(m.proj)
     exchange_arrived(m.in1, recv.in1)
 
     for s in range(OWN):
@@ -449,7 +446,7 @@
     def other_bias_arrived(hh):
         arrived(m.bias.at[(1 - e) * 2 + hh], recv.partner.at[hh])
 
-    def attend(h):
+    def attend(h, then=None):
         here = pl.ds(pl.multiple_of(h * DH, DH), DH)
         lane = lax.div(lax.broadcasted_iota(jnp.int32, (C, C), 1), DH)
         by_lane = (lane == h).astype(F32).astype(BF16)
@@ -476,6 +473,8 @@
                 dk_sum = dk_part if dk_sum is None else dk_sum + dk_part
             m.dk[s] += dk_sum
             m.dv[s] += dv_sum
+            if then is not None:
+                then(s)
             return carry
 
         lax.fori_loop(0, OWN, one_row, 0)
@@ -524,6 +523,23 @@
             arrived(m.d_near_in.at[hh, n], recv.d_near.at[hh, n])
         return (m.d_near[hh, at.f] + m.d_near_in[hh, 0]) + (m.d_near_in[hh, 1] + m.d_near_in[hh, 2])
 
+    def finish_row(s):
+        attended = m.att_t[s].T
+        gated = (m.gate[s] * attended).astype(BF16)
+        pair_mask = m.mask[...].reshape(N, C) * m.row_mask[s]
+        update = jnp.dot(gated, w_out[...], preferred_element_type=F32) * pair_mask
+        d_proj = jnp.concatenate(
+            [m.dq_t[s].T * SCALE, m.dk[s], m.dv[s], m.dgate[s] * attended], axis=1
+        ).astype(BF16)
+        d_normed = lax.dot_general(d_proj, w_proj[...], NT, preferred_element_type=F32)
+        result = norm_backward(d_normed * gain[...], m.unit[s], m.rstd[s])
+        m.out[s] = jnp.concatenate(
+            [update.reshape(COLS, WIDTH, C), result.reshape(COLS, WIDTH, C)], axis=1
+        ).astype(BF16)
+        exchange_start(at, m.out.at[s], land.at[at.c, s], send.out.at[s], recv.out.at[s])
+        normed_t = m.normed[s].astype(F32).T.astype(BF16)
+        m.proj[...] += jnp.dot(normed_t, d_proj, preferred_element_type=F32)
+
     own_bias_arrived(0)
     attend(e * 2)
     own_bias_arrived(1)
@@ -534,51 +550,23 @@
     attend(3 - e * 2)
     to_other(1)
     scatter_far(0)
-    attend(e * 2 + 1)
+    attend(e * 2 + 1, finish_row)
     scatter_far(1)
 
-    for s in range(OWN):
-        attended = m.att_t[s].T
-        m.att[s] = attended
-        d_proj = jnp.concatenate(
-            [m.dq_t[s].T * SCALE, m.dk[s], m.dv[s], m.dgate[s] * attended], axis=1
-        ).astype(BF16)
-        m.d_proj[s] = d_proj
-        normed_t = m.normed[s].astype(F32).T.astype(BF16)
-        share = jnp.dot(normed_t, d_proj, preferred_element_type=F32)
-        if s == 0:
-            m.proj[...] = share
-        else:
-            m.proj[...] += share
-
-    def rows_of(ref, c):
-        return ref.at[pl.ds(pl.multiple_of(c * 8, 8), 8), :]
+    def piece(ref, c):
+        rows = pl.ds(pl.multiple_of(lax.div(c, 2) * 16, 16), 16)
+        return ref.at[rows, pl.ds(pl.multiple_of(lax.rem(c, 2) * 2 * HD, 2 * HD), 2 * HD)]
+
+    m.proj_b[...] = m.proj[...].astype(BF16)
 
     def scatter_proj(n, carry):
         t = lax.rem(at.c + n, COLS)
-        remote(rows_of(m.proj, t), m.r5.at[n], send.p1.at[n], recv.p1.at[n], at.plane(n)).start()
+        remote(piece(m.proj_b, t), m.r5.at[n], send.p1.at[n], recv.p1.at[n], at.plane(n)).start()
         return carry
 
     lax.fori_loop(1, COLS, scatter_proj, 0)
     scatter_near(0)
-
-    for s in range(OWN):
-        gated = (m.gate[s] * m.att[s]).astype(BF16)
-        pair_mask = m.mask[...].reshape(N, C) * m.row_mask[s]
-        update = jnp.dot(gated, w_out[...], preferred_element_type=F32) * pair_mask
-        m.stage_u[:, s * WIDTH : (s + 1) * WIDTH, :] = update.reshape(COLS, WIDTH, C)
-    m.stage_u[:, PART:, :] = pad
-    m.out_u[...] = m.stage_u[...].astype(BF16)
-    exchange_start(at, m.out_u, land_u, send.u, recv.u)
     scatter_near(1)
-
-    for s in range(OWN):
-        d_normed = lax.dot_general(m.d_proj[s], w_proj[...], NT, preferred_element_type=F32)
-        result = norm_backward(d_normed * gain[...], m.unit[s], m.rstd[s])
-        m.stage_a[:, s * WIDTH : (s + 1) * WIDTH, :] = result.reshape(COLS, WIDTH, C)
-    m.stage_a[:, PART:, :] = pad
-    m.out_a[...] = m.stage_a[...].astype(BF16)
-    exchange_start(at, m.out_a, land_a, send.a, recv.a)
 
     halves = [plane_sum(0), plane_sum(1)]
     blank = jnp.zeros((WIDTH, SLOT - TALL), F32)
@@ -602,9 +590,9 @@
 
     def proj_arrived(n, total):
         arrived(m.r5.at[n], recv.p1.at[n])
-        return total + m.r5[n]
-
-    m.v5[...] = lax.fori_loop(1, COLS, proj_arrived, m.proj[pl.ds(pl.multiple_of(at.c * 8, 8), 8), :])
+        return total + m.r5[n].astype(F32)
+
+    m.v5[...] = lax.fori_loop(1, COLS, proj_arrived, piece(m.proj, at.c)[...])
 
     def proj_to_homes(z, carry):
         slot = e * 4 + at.zz
@@ -617,12 +605,12 @@
         arrived(m.r6.at[n], recv.p2.at[n])
         return total + m.r6[n]
 
-    m.v6[...] = lax.fori_loop(0, 8, share_arrived, jnp.zeros((8, 4 * HD), F32))
-    own_rows = rows_of(proj_out, at.c)
-    pltpu.make_async_copy(m.v6, own_rows, recv.p3.at[0]).start()
+    m.v6[...] = lax.fori_loop(0, 8, share_arrived, jnp.zeros((16, 2 * HD), F32)).astype(BF16)
+    own_piece = piece(proj_out, at.c)
+    pltpu.make_async_copy(m.v6, own_piece, recv.p3.at[0]).start()
 
     def spread(n, carry):
-        remote(m.v6, own_rows, send.p3.at[n], recv.p3.at[n], at.plane(n)).start()
+        remote(m.v6, own_piece, send.p3.at[n], recv.p3.at[n], at.plane(n)).start()
         return carry
 
     lax.fori_loop(1, COLS, spread, 0)
@@ -632,11 +620,11 @@
             arrived(m.hin.at[core, zz], recv.dz.at[core * 4 + zz])
         lanes = slice(core * PAIR, (core + 1) * PAIR)
         h_sum[:, lanes] = (m.hin[core, 0] + m.hin[core, 1]) + (m.hin[core, 2] + m.hin[core, 3])
-    exchange_arrived(land_u, recv.u)
-    exchange_arrived(land_a, recv.a)
+    for s in range(OWN):
+        exchange_arrived(land.at[:, s], recv.out.at[s])
 
     def out_arrived(n, carry):
-        arrived(rows_of(proj_out, lax.rem(at.c - n + COLS, COLS)), recv.p3.at[n])
+        arrived(piece(proj_out, lax.rem(at.c - n + COLS, COLS)), recv.p3.at[n])
         return carry
 
     lax.fori_loop(0, COLS, out_arrived, 0)
@@ -645,7 +633,7 @@
     arrived(rstd_out, recv.norm.at[1])
 
     def column_sent(n, carry):
-        arrived(m.v5, send.p1.at[n])
+        arrived(m.v6, send.p1.at[n])
         arrived(m.v6, send.p3.at[n])
         return carry
 
@@ -675,22 +663,22 @@
         arrived(m.d_bias.at[0], send.back.at[hh])
     exchange_sent(at, m.m1, send.in1)
     exchange_sent(at, m.m2, send.in2)
-    exchange_sent(at, m.out_u, send.u)
-    exchange_sent(at, m.out_a, send.a)
+    for s in range(OWN):
+        exchange_sent(at, m.out.at[s], send.out.at[s])
 
 
 STEPS = 4
 
 
 def finish_kernel(
-    land_u, land_a, proj_in, h_sum, unit, rstd, gain, w_bias_t, update, pair_grad, proj_out, w_rep, split, share
+    land, proj_in, h_sum, unit, rstd, gain, w_bias_t, update, pair_grad, proj_out, w_rep, split, share
 ):
     tall = TALL // STEPS
     step = pl.program_id(0)
 
     @pl.when(step == 0)
     def _():
-        proj_out[...] = proj_in[...]
+        proj_out[...] = proj_in[...].astype(F32)
         w_rep[...] = repeat_heads(w_bias_t)
         total = h_sum[...]
         for n in range(3):
@@ -698,8 +686,9 @@
             split[n * WIDTH : (n + 1) * WIDTH, :] = term
             total = total - term
 
-    update[...] = land_u[:, :PART, :].astype(F32).reshape(tall, WIDTH, C).astype(BF16)
-    share[...] = land_a[:, :PART, :].astype(F32).reshape(tall, WIDTH, C)
+    landed = land[...].astype(F32)
+    update[...] = landed[:, :, :WIDTH, :].reshape(tall, WIDTH, C).astype(BF16)
+    share[...] = landed[:, :, WIDTH:, :].reshape(tall, WIDTH, C)
     terms = split[...].astype(BF16)
     for i in range(tall):
         parts = lax.dot_general(
@@ -720,21 +709,20 @@
     any_space = pl.BlockSpec(memory_space=pl.ANY)
     gain = ln_gain.reshape(1, C)
     sems = [pltpu.SemaphoreType.DMA(shape) for shape in MAIN_SEMS.values()]
-    landing = jax.ShapeDtypeStruct((COLS, PADDED, C), BF16)
+    landing = jax.ShapeDtypeStruct((COLS, OWN, 2 * WIDTH, C), BF16)
     block = jax.ShapeDtypeStruct(pair_act.shape, F32)
     proj_shape = jax.ShapeDtypeStruct((C, 4 * HD), F32)
-    land_u, land_a, proj, h_sum, unit, rstd = pl.pallas_call(
+    land, proj, h_sum, unit, rstd = pl.pallas_call(
         main_kernel,
         out_shape=[
             landing,
-            landing,
-            proj_shape,
+            jax.ShapeDtypeStruct((C, 4 * HD), BF16),
             jax.ShapeDtypeStruct((WIDTH, H * SLOT), F32),
             block,
             block,
         ],
         in_specs=[pl.BlockSpec(memory_space=pltpu.SMEM)] + [any_space] * (MAIN_IN - 1),
-        out_specs=[any_space] * 3 + vmem(1) + [any_space] * 2,
+        out_specs=[any_space] * 2 + vmem(1) + [any_space] * 2,
         scratch_shapes=[pltpu.VMEM(shape, dtype) for shape, dtype in MAIN_SCRATCH.values()] + sems + sems,
         compiler_params=pltpu.CompilerParams(
             collective_id=0, has_side_effects=True, vmem_limit_bytes=VMEM_LIMIT
@@ -755,7 +743,7 @@
     result = jax.ShapeDtypeStruct(pair_act.shape, BF16)
     tall = TALL // STEPS
     rows = pl.BlockSpec((tall, WIDTH, C), lambda n: (n, 0, 0))
-    landed = pl.BlockSpec((COLS // STEPS, PADDED, C), lambda n: (n, 0, 0))
+    landed = pl.BlockSpec((COLS // STEPS, OWN, 2 * WIDTH, C), lambda n: (n, 0, 0, 0))
 
     def whole(*shape):
         return pl.BlockSpec(shape, lambda n: (0,) * len(shape))
@@ -765,7 +753,6 @@
         out_shape=[result, result, proj_shape],
         grid=(STEPS,),
         in_specs=[
-            landed,
             landed,
             whole(C, 4 * HD),
             whole(WIDTH, H * SLOT),
@@ -782,7 +769,7 @@
         ],
         compiler_params=pltpu.CompilerParams(vmem_limit_bytes=VMEM_LIMIT),
         name="finish",
-    )(land_u, land_a, proj, h_sum, unit, rstd, gain, w_bias.T)
+    )(land, proj, h_sum, unit, rstd, gain, w_bias.T)
 
 
 def solution(mesh):

time: 82.7 us -> 80.9 us (0.978)
  Pallas kernels: 81.3 us -> 79.4 us
    pallas_call x1, Pallas kernels: 76.4 us -> 74.6 us  [shards(): pl.pallas_call(main_kernel, out_shape=[landing, jax.ShapeDtypeStruct((C,...]
where the time goes in v5:
time: 80.9 us; the launch traced here: 80.7 us
  Pallas kernels  79.4 us (98%)
  between operations  1.29 us (2%)
    pallas_call x1, Pallas kernels, shards(): pl.pallas_call(main_kernel, out_shape=[landing, jax.ShapeDtypeStruct((C,...  74.6 us
    pallas_call x1, Pallas kernels, shards(): pl.pallas_call(finish_kernel, out_shape=[result, result, proj_shape], gri...  4.8 us

profile of v5, /device:TPU:1, one launch (start us, length us, event | category | flops | bytes accessed | tf_op | source)
XLA Modules:
  0.0 80.7 jit_solution(8169286451297098350)
XLA Ops:
  1.3 74.6 %main.1 = (bf16[16,3,48,128]{3,2,1,0:T(8,128)(2,1)}, bf16[128,512]{1,0:T(8,128)(2,1)}, f32[24,256]{1,0:T(8,128)}, f32[48,24,128]{2,1,0:T(8,128)}, f32[48,24,128]{2,1,0:T(8,128)}) custom-call(s32[1]{0:T(128)S(6)} %copy.13.refs_0_, bf16[48,24,128]{2,1,0:T(8,128)(2,1)} %refs_1_.1, bf16[48,24,128]{2,1,0:T(8,128)(2,1)} %refs_2_.1, s32[1,24]{1,0:T(1,128)} %bitcast.9, ...), custom_call_target="tpu_custom_call" | custom-call | tf_op jit(solution)/shard_map/main/pallas_call | solution.py:715
  75.9 4.8 %finish.1 = (bf16[48,24,128]{2,1,0:T(8,128)(2,1)}, bf16[48,24,128]{2,1,0:T(8,128)(2,1)}, f32[128,512]{1,0:T(8,128)}) custom-call(bf16[16,3,48,128]{3,2,1,0:T(8,128)(2,1)} %get-tuple-element.8.land, bf16[128,512]{1,0:T(8,128)(2,1)} %get-tuple-element.9.proj_in, f32[24,256]{1,0:T(8,128)} %get-tuple-element.10.h_sum, f32[48,24,128]{2,1,0:T(8,128)} %get-tuple-element.11.unit, ...), custom_call_target="tpu_custom_call" | custom-call | tf_op jit(solution)/shard_map/finish/pallas_call | solution.py:751

commit v6 on v5

--- a/solution.py
+++ b/solution.py
@@ -536,7 +536,6 @@
         m.out[s] = jnp.concatenate(
             [update.reshape(COLS, WIDTH, C), result.reshape(COLS, WIDTH, C)], axis=1
         ).astype(BF16)
-        exchange_start(at, m.out.at[s], land.at[at.c, s], send.out.at[s], recv.out.at[s])
         normed_t = m.normed[s].astype(F32).T.astype(BF16)
         m.proj[...] += jnp.dot(normed_t, d_proj, preferred_element_type=F32)
 
@@ -568,6 +567,21 @@
     scatter_near(0)
     scatter_near(1)
 
+    def proj_arrived(n, total):
+        arrived(m.r5.at[n], recv.p1.at[n])
+        return total + m.r5[n].astype(F32)
+
+    m.v5[...] = lax.fori_loop(1, COLS, proj_arrived, piece(m.proj, at.c)[...])
+
+    def proj_to_homes(z, carry):
+        slot = e * 4 + at.zz
+        send_or_copy(at.is_home(z), m.v5, m.r6.at[slot], send.p2.at[z], recv.p2.at[slot], at.home(z))
+        return carry
+
+    lax.fori_loop(0, ROWS, proj_to_homes, 0)
+
+    for s in range(OWN):
+        exchange_start(at, m.out.at[s], land.at[at.c, s], send.out.at[s], recv.out.at[s])
     halves = [plane_sum(0), plane_sum(1)]
     blank = jnp.zeros((WIDTH, SLOT - TALL), F32)
     for z in range(ROWS):
@@ -587,19 +601,6 @@
 
     lax.fori_loop(0, ROWS, to_homes, 0)
 
-
-    def proj_arrived(n, total):
-        arrived(m.r5.at[n], recv.p1.at[n])
-        return total + m.r5[n].astype(F32)
-
-    m.v5[...] = lax.fori_loop(1, COLS, proj_arrived, piece(m.proj, at.c)[...])
-
-    def proj_to_homes(z, carry):
-        slot = e * 4 + at.zz
-        send_or_copy(at.is_home(z), m.v5, m.r6.at[slot], send.p2.at[z], recv.p2.at[slot], at.home(z))
-        return carry
-
-    lax.fori_loop(0, ROWS, proj_to_homes, 0)
 
     def share_arrived(n, total):
         arrived(m.r6.at[n], recv.p2.at[n])
@@ -667,7 +668,7 @@
         exchange_sent(at, m.out.at[s], send.out.at[s])
 
 
-STEPS = 4
+STEPS = 2
 
 
 def finish_kernel(

time: 80.9 us -> 74 us (0.915)
  Pallas kernels: 79.4 us -> 72.6 us
    pallas_call x1, Pallas kernels: 74.6 us -> 68.8 us  [shards(): pl.pallas_call(main_kernel, out_shape=[landing, jax.ShapeDtypeStruct((C,...]
    pallas_call x1, Pallas kernels: 4.8 us -> 3.8 us  [shards(): pl.pallas_call(finish_kernel, out_shape=[result, result, proj_shape], gri...]
where the time goes in v6:
time: 74 us; the launch traced here: 73.9 us
  Pallas kernels  72.6 us (98%)
  between operations  1.29 us (2%)
    pallas_call x1, Pallas kernels, shards(): pl.pallas_call(main_kernel, out_shape=[landing, jax.ShapeDtypeStruct((C,...  68.8 us
    pallas_call x1, Pallas kernels, shards(): pl.pallas_call(finish_kernel, out_shape=[result, result, proj_shape], gri...  3.8 us

profile of v6, /device:TPU:1, one launch (start us, length us, event | category | flops | bytes accessed | tf_op | source)
XLA Modules:
  0.0 73.9 jit_solution(13975129692620026191)
XLA Ops:
  1.3 68.8 %main.1 = (bf16[16,3,48,128]{3,2,1,0:T(8,128)(2,1)}, bf16[128,512]{1,0:T(8,128)(2,1)}, f32[24,256]{1,0:T(8,128)}, f32[48,24,128]{2,1,0:T(8,128)}, f32[48,24,128]{2,1,0:T(8,128)}) custom-call(s32[1]{0:T(128)S(6)} %copy.13.refs_0_, bf16[48,24,128]{2,1,0:T(8,128)(2,1)} %refs_1_.1, bf16[48,24,128]{2,1,0:T(8,128)(2,1)} %refs_2_.1, s32[1,24]{1,0:T(1,128)} %bitcast.9, ...), custom_call_target="tpu_custom_call" | custom-call | tf_op jit(solution)/shard_map/main/pallas_call | solution.py:716
  70.0 3.8 %finish.1 = (bf16[48,24,128]{2,1,0:T(8,128)(2,1)}, bf16[48,24,128]{2,1,0:T(8,128)(2,1)}, f32[128,512]{1,0:T(8,128)}) custom-call(bf16[16,3,48,128]{3,2,1,0:T(8,128)(2,1)} %get-tuple-element.8.land, bf16[128,512]{1,0:T(8,128)(2,1)} %get-tuple-element.9.proj_in, f32[24,256]{1,0:T(8,128)} %get-tuple-element.10.h_sum, f32[48,24,128]{2,1,0:T(8,128)} %get-tuple-element.11.unit, ...), custom_call_target="tpu_custom_call" | custom-call | tf_op jit(solution)/shard_map/finish/pallas_call | solution.py:752

commit v7 on v6

--- a/solution.py
+++ b/solution.py
@@ -355,7 +355,6 @@
     pltpu.make_async_copy(m.home_rstd, rstd_out, recv.norm.at[1]).start()
 
     m.w_proj_t[...] = w_proj[:, : 3 * HD].astype(F32).T.astype(BF16)
-    m.d_bias[...] = jnp.zeros_like(m.d_bias)
     m.dk[...] = jnp.zeros_like(m.dk)
     m.dv[...] = jnp.zeros_like(m.dv)
     m.proj[...] = jnp.zeros_like(m.proj)
@@ -446,38 +445,37 @@
     def other_bias_arrived(hh):
         arrived(m.bias.at[(1 - e) * 2 + hh], recv.partner.at[hh])
 
-    def attend(h, then=None):
+    def attend(h):
         here = pl.ds(pl.multiple_of(h * DH, DH), DH)
-        lane = lax.div(lax.broadcasted_iota(jnp.int32, (C, C), 1), DH)
+        lane = lax.div(lax.broadcasted_iota(jnp.int32, (1, C), 1), DH)
         by_lane = (lane == h).astype(F32).astype(BF16)
-
-        def one_row(s, carry):
-            keys_t, values_t = m.k_t[s, here, :], m.v_t[s, here, :]
-            dk_sum = dv_sum = None
-            for n in range(3):
-                lanes = slice(n * C, (n + 1) * C)
+        dk, dv = [None] * OWN, [None] * OWN
+        for n in range(3):
+            lanes = slice(n * C, (n + 1) * C)
+            d_bias = None
+            for s in range(OWN):
                 scores = m.scores[h, s, :, lanes] + m.bias[h, :, :, lanes].reshape(N, C)
                 exponent = jnp.exp(scores - jnp.max(scores, axis=0, keepdims=True))
                 weights = exponent * (1.0 / jnp.sum(exponent, axis=0, keepdims=True))
                 weights_b = weights.astype(BF16)
-                attended = jnp.dot(values_t, weights_b, preferred_element_type=F32)
-                m.att_t[s, here, lanes] = attended
-                delta = jnp.sum(attended * m.d_t[s, here, lanes].astype(F32), axis=0, keepdims=True)
-                d_score = weights * (m.d_prob[h, s, :, lanes] - delta)
+                m.att_t[s, here, lanes] = jnp.dot(
+                    m.v_t[s, here, :], weights_b, preferred_element_type=F32
+                )
+                d_prob = m.d_prob[h, s, :, lanes]
+                d_score = weights * (d_prob - jnp.sum(weights * d_prob, axis=0, keepdims=True))
                 d_score_b = d_score.astype(BF16)
-                m.d_bias[h, :, :, lanes] += d_score.reshape(COLS, WIDTH, C)
-                m.dq_t[s, here, lanes] = jnp.dot(keys_t, d_score_b, preferred_element_type=F32)
+                d_bias = d_score if d_bias is None else d_bias + d_score
+                m.dq_t[s, here, lanes] = jnp.dot(
+                    m.k_t[s, here, :], d_score_b, preferred_element_type=F32
+                )
                 dv_part = jnp.dot(weights_b, m.d[s, lanes, :] * by_lane, preferred_element_type=F32)
                 dk_part = jnp.dot(d_score_b, m.q[s, lanes, :] * by_lane, preferred_element_type=F32)
-                dv_sum = dv_part if dv_sum is None else dv_sum + dv_part
-                dk_sum = dk_part if dk_sum is None else dk_sum + dk_part
-            m.dk[s] += dk_sum
-            m.dv[s] += dv_sum
-            if then is not None:
-                then(s)
-            return carry
-
-        lax.fori_loop(0, OWN, one_row, 0)
+                dv[s] = dv_part if dv[s] is None else dv[s] + dv_part
+                dk[s] = dk_part if dk[s] is None else dk[s] + dk_part
+            m.d_bias[h, :, :, lanes] = d_bias.reshape(COLS, WIDTH, C)
+        for s in range(OWN):
+            m.dk[s] += dk[s]
+            m.dv[s] += dv[s]
 
     def to_other(hh):
         head = (1 - e) * 2 + hh
@@ -549,8 +547,10 @@
     attend(3 - e * 2)
     to_other(1)
     scatter_far(0)
-    attend(e * 2 + 1, finish_row)
+    attend(e * 2 + 1)
     scatter_far(1)
+    for s in range(OWN):
+        finish_row(s)
 
     def piece(ref, c):
         rows = pl.ds(pl.multiple_of(lax.div(c, 2) * 16, 16), 16)

time: 74 us -> 69.1 us (0.934)
  Pallas kernels: 72.6 us -> 67.6 us
    pallas_call x1, Pallas kernels: 68.8 us -> 63.8 us  [shards(): pl.pallas_call(main_kernel, out_shape=[landing, jax.ShapeDtypeStruct((C,...]
where the time goes in v7:
time: 69.1 us; the launch traced here: 68.9 us
  Pallas kernels  67.6 us (98%)
  between operations  1.29 us (2%)
    pallas_call x1, Pallas kernels, shards(): pl.pallas_call(main_kernel, out_shape=[landing, jax.ShapeDtypeStruct((C,...  63.8 us
    pallas_call x1, Pallas kernels, shards(): pl.pallas_call(finish_kernel, out_shape=[result, result, proj_shape], gri...  3.8 us

profile of v7, /device:TPU:1, one launch (start us, length us, event | category | flops | bytes accessed | tf_op | source)
XLA Modules:
  0.0 68.9 jit_solution(2742302328914595649)
XLA Ops:
  1.3 63.8 %main.1 = (bf16[16,3,48,128]{3,2,1,0:T(8,128)(2,1)}, bf16[128,512]{1,0:T(8,128)(2,1)}, f32[24,256]{1,0:T(8,128)}, f32[48,24,128]{2,1,0:T(8,128)}, f32[48,24,128]{2,1,0:T(8,128)}) custom-call(s32[1]{0:T(128)S(6)} %copy.13.refs_0_, bf16[48,24,128]{2,1,0:T(8,128)(2,1)} %refs_1_.1, bf16[48,24,128]{2,1,0:T(8,128)(2,1)} %refs_2_.1, s32[1,24]{1,0:T(1,128)} %bitcast.9, ...), custom_call_target="tpu_custom_call" | custom-call | tf_op jit(solution)/shard_map/main/pallas_call | solution.py:716
  65.1 3.8 %finish.1 = (bf16[48,24,128]{2,1,0:T(8,128)(2,1)}, bf16[48,24,128]{2,1,0:T(8,128)(2,1)}, f32[128,512]{1,0:T(8,128)}) custom-call(bf16[16,3,48,128]{3,2,1,0:T(8,128)(2,1)} %get-tuple-element.8.land, bf16[128,512]{1,0:T(8,128)(2,1)} %get-tuple-element.9.proj_in, f32[24,256]{1,0:T(8,128)} %get-tuple-element.10.h_sum, f32[48,24,128]{2,1,0:T(8,128)} %get-tuple-element.11.unit, ...), custom_call_target="tpu_custom_call" | custom-call | tf_op jit(solution)/shard_map/finish/pallas_call | solution.py:752

commit v8 on v7

--- a/solution.py
+++ b/solution.py
@@ -248,7 +248,7 @@
     v5=((16, 2 * HD), F32),
     r6=((8, 16, 2 * HD), F32),
     v6=((16, 2 * HD), BF16),
-    out=((OWN, COLS, 2 * WIDTH, C), BF16),
+    out=((COLS, OWN, 2 * WIDTH, C), BF16),
 )
 MAIN_SEMS = dict(
     operand=(9,),
@@ -266,7 +266,7 @@
     p1=(COLS,),
     p2=(8,),
     p3=(COLS,),
-    out=(OWN, COLS),
+    out=(2, COLS),
 )
 MAIN_IN = 10
 MAIN_OUT = 5
@@ -303,6 +303,38 @@
     valid = jnp.where(lane + at.c * WIDTH < length[0], residues[...], 0).astype(F32)
     valid = jnp.sum(jnp.where(lane == sublane, valid, 0.0), axis=1, keepdims=True)
     m.flags[...] = jnp.broadcast_to(valid, (WIDTH, C))
+    m.w_rep[...] = repeat_heads(w_bias_t)
+    unit, inverse = standardize(pair[...].astype(F32).reshape(TALL * WIDTH, C))
+    m.home_unit[...] = unit.reshape(TALL, WIDTH, C)
+    m.home_rstd[...] = inverse.reshape(TALL, WIDTH, C)
+    m.home_rows[...] = (unit * gain[...] + shift[...]).reshape(TALL, WIDTH, C)
+
+    def home_bias(n, total):
+        for i in range(8):
+            rows = m.home_rows[n * 8 + i].astype(BF16)
+            total = total + jnp.dot(rows, only_row(m.w_rep[...], n * 8 + i), preferred_element_type=F32)
+        return total
+
+    packed = lax.fori_loop(0, TALL // 8, home_bias, jnp.zeros((WIDTH, H * SLOT), F32))
+    negative = (m.flags[...] - 1.0) * 1e9
+    m.zpack[0] = packed[:, :PAIR] + negative
+    m.zpack[1] = packed[:, PAIR:] + negative
+
+    pl.semaphore_wait(pltpu.get_barrier_semaphore(), count)
+
+    def to_workers(n, carry):
+        core, zz = lax.div(n, 4), lax.rem(n, 4)
+        send_or_copy(
+            at.is_worker(core, zz),
+            m.zpack.at[core],
+            m.zin.at[at.z],
+            send.z.at[n],
+            recv.z.at[at.z],
+            at.worker(core, zz),
+        )
+        return carry
+
+    lax.fori_loop(0, 8, to_workers, 0)
     lane = lax.broadcasted_iota(jnp.int32, (8, C), 1)
     packed_flags = jnp.where(
         lane == 0, m.flags[0:8, :], jnp.where(lane == 1, m.flags[8:16, :], m.flags[16:24, :])
@@ -317,38 +349,6 @@
     ).astype(BF16)
     m.m2[...] = jnp.concatenate([cot[...].astype(F32).reshape(COLS, PART, C), pad], axis=1).astype(BF16)
 
-    m.w_rep[...] = repeat_heads(w_bias_t)
-    unit, inverse = standardize(pair[...].astype(F32).reshape(TALL * WIDTH, C))
-    m.home_unit[...] = unit.reshape(TALL, WIDTH, C)
-    m.home_rstd[...] = inverse.reshape(TALL, WIDTH, C)
-    m.home_rows[...] = (unit * gain[...] + shift[...]).reshape(TALL, WIDTH, C)
-
-    def home_bias(n, total):
-        for i in range(8):
-            rows = m.home_rows[n * 8 + i].astype(BF16)
-            total = total + jnp.dot(rows, only_row(m.w_rep[...], n * 8 + i), preferred_element_type=F32)
-        return total
-
-    packed = lax.fori_loop(0, TALL // 8, home_bias, jnp.zeros((WIDTH, H * SLOT), F32))
-    negative = (m.flags[...] - 1.0) * 1e9
-    m.zpack[0] = packed[:, :PAIR] + negative
-    m.zpack[1] = packed[:, PAIR:] + negative
-
-    pl.semaphore_wait(pltpu.get_barrier_semaphore(), count)
-
-    def to_workers(n, carry):
-        core, zz = lax.div(n, 4), lax.rem(n, 4)
-        send_or_copy(
-            at.is_worker(core, zz),
-            m.zpack.at[core],
-            m.zin.at[at.z],
-            send.z.at[n],
-            recv.z.at[at.z],
-            at.worker(core, zz),
-        )
-        return carry
-
-    lax.fori_loop(0, 8, to_workers, 0)
     exchange_start(at, m.m1, m.in1.at[at.c], send.in1, recv.in1)
     exchange_start(at, m.m2, m.in2.at[at.c], send.in2, recv.in2)
     pltpu.make_async_copy(m.home_unit, unit_out, recv.norm.at[0]).start()
@@ -358,15 +358,6 @@
     m.dk[...] = jnp.zeros_like(m.dk)
     m.dv[...] = jnp.zeros_like(m.dv)
     m.proj[...] = jnp.zeros_like(m.proj)
-    exchange_arrived(m.in1, recv.in1)
-
-    for s in range(OWN):
-        values = m.in1[:, s * WIDTH : (s + 1) * WIDTH, :].astype(F32).reshape(N, C)
-        unit, inverse = standardize(values)
-        m.unit[s] = unit
-        m.rstd[s] = inverse
-        m.normed[s] = (unit * gain[...] + shift[...]).astype(BF16)
-
     def bias_block(hh, a, b):
         return m.bias.at[e * 2 + hh, at.col(at.f - a + 4, at.g - b + 4)]
 
@@ -392,6 +383,17 @@
             remote(mine, mine, send.near.at[hh, n - 1], recv.near.at[hh, n - 1], at.fpeer(n)).start()
         to_far(hh, 0)
 
+    forward(0)
+    forward(1)
+    exchange_arrived(m.in1, recv.in1)
+
+    for s in range(OWN):
+        values = m.in1[:, s * WIDTH : (s + 1) * WIDTH, :].astype(F32).reshape(N, C)
+        unit, inverse = standardize(values)
+        m.unit[s] = unit
+        m.rstd[s] = inverse
+        m.normed[s] = (unit * gain[...] + shift[...]).astype(BF16)
+
     for s in range(OWN):
         rows = m.normed[s]
         flat = jnp.dot(rows, w_proj[...], preferred_element_type=F32)
@@ -404,8 +406,6 @@
         m.k_t[s] = flat_t[HD : 2 * HD].astype(BF16)
         m.v_t[s] = flat_t[2 * HD : 3 * HD].astype(BF16)
 
-    forward(0)
-    forward(1)
     exchange_arrived(m.in2, recv.in2)
     tiles = m.in1[:, PART:, :].astype(F32)
     for t in range(3):
@@ -531,11 +531,17 @@
         ).astype(BF16)
         d_normed = lax.dot_general(d_proj, w_proj[...], NT, preferred_element_type=F32)
         result = norm_backward(d_normed * gain[...], m.unit[s], m.rstd[s])
-        m.out[s] = jnp.concatenate(
+        m.out[:, s] = jnp.concatenate(
             [update.reshape(COLS, WIDTH, C), result.reshape(COLS, WIDTH, C)], axis=1
         ).astype(BF16)
         normed_t = m.normed[s].astype(F32).T.astype(BF16)
         m.proj[...] += jnp.dot(normed_t, d_proj, preferred_element_type=F32)
+
+    def back(n):
+        rows = pl.ds(0, 2) if n == 0 else pl.ds(2, 1)
+        exchange_start(
+            at, m.out.at[:, rows], land.at[at.c, rows], send.out.at[n], recv.out.at[n]
+        )
 
     own_bias_arrived(0)
     attend(e * 2)
@@ -565,6 +571,7 @@
 
     lax.fori_loop(1, COLS, scatter_proj, 0)
     scatter_near(0)
+    back(0)
     scatter_near(1)
 
     def proj_arrived(n, total):
@@ -580,8 +587,7 @@
 
     lax.fori_loop(0, ROWS, proj_to_homes, 0)
 
-    for s in range(OWN):
-        exchange_start(at, m.out.at[s], land.at[at.c, s], send.out.at[s], recv.out.at[s])
+    back(1)
     halves = [plane_sum(0), plane_sum(1)]
     blank = jnp.zeros((WIDTH, SLOT - TALL), F32)
     for z in range(ROWS):
@@ -621,8 +627,8 @@
             arrived(m.hin.at[core, zz], recv.dz.at[core * 4 + zz])
         lanes = slice(core * PAIR, (core + 1) * PAIR)
         h_sum[:, lanes] = (m.hin[core, 0] + m.hin[core, 1]) + (m.hin[core, 2] + m.hin[core, 3])
-    for s in range(OWN):
-        exchange_arrived(land.at[:, s], recv.out.at[s])
+    exchange_arrived(land.at[:, pl.ds(0, 2)], recv.out.at[0])
+    exchange_arrived(land.at[:, pl.ds(2, 1)], recv.out.at[1])
 
     def out_arrived(n, carry):
         arrived(piece(proj_out, lax.rem(at.c - n + COLS, COLS)), recv.p3.at[n])
@@ -664,8 +670,8 @@
         arrived(m.d_bias.at[0], send.back.at[hh])
     exchange_sent(at, m.m1, send.in1)
     exchange_sent(at, m.m2, send.in2)
-    for s in range(OWN):
-        exchange_sent(at, m.out.at[s], send.out.at[s])
+    exchange_sent(at, m.out.at[:, pl.ds(0, 2)], send.out.at[0])
+    exchange_sent(at, m.out.at[:, pl.ds(2, 1)], send.out.at[1])
 
 
 STEPS = 2

time: 69.1 us -> 64.3 us (0.931)
  Pallas kernels: 67.6 us -> 62.7 us
    pallas_call x1, Pallas kernels: 63.8 us -> 58.9 us  [shards(): pl.pallas_call(main_kernel, out_shape=[landing, jax.ShapeDtypeStruct((C,...]
where the time goes in v8:
time: 64.3 us; the launch traced here: 64 us
  Pallas kernels  62.7 us (98%)
  between operations  1.29 us (2%)
    pallas_call x1, Pallas kernels, shards(): pl.pallas_call(main_kernel, out_shape=[landing, jax.ShapeDtypeStruct((C,...  58.9 us
    pallas_call x1, Pallas kernels, shards(): pl.pallas_call(finish_kernel, out_shape=[result, result, proj_shape], gri...  3.8 us

profile of v8, /device:TPU:1, one launch (start us, length us, event | category | flops | bytes accessed | tf_op | source)
XLA Modules:
  0.0 64.0 jit_solution(15614355242348279861)
XLA Ops:
  1.3 58.9 %main.1 = (bf16[16,3,48,128]{3,2,1,0:T(8,128)(2,1)}, bf16[128,512]{1,0:T(8,128)(2,1)}, f32[24,256]{1,0:T(8,128)}, f32[48,24,128]{2,1,0:T(8,128)}, f32[48,24,128]{2,1,0:T(8,128)}) custom-call(s32[1]{0:T(128)S(6)} %copy.13.refs_0_, bf16[48,24,128]{2,1,0:T(8,128)(2,1)} %refs_1_.1, bf16[48,24,128]{2,1,0:T(8,128)(2,1)} %refs_2_.1, s32[1,24]{1,0:T(1,128)} %bitcast.9, ...), custom_call_target="tpu_custom_call" | custom-call | tf_op jit(solution)/shard_map/main/pallas_call | solution.py:722
  60.2 3.8 %finish.1 = (bf16[48,24,128]{2,1,0:T(8,128)(2,1)}, bf16[48,24,128]{2,1,0:T(8,128)(2,1)}, f32[128,512]{1,0:T(8,128)}) custom-call(bf16[16,3,48,128]{3,2,1,0:T(8,128)(2,1)} %get-tuple-element.8.land, bf16[128,512]{1,0:T(8,128)(2,1)} %get-tuple-element.9.proj_in, f32[24,256]{1,0:T(8,128)} %get-tuple-element.10.h_sum, f32[48,24,128]{2,1,0:T(8,128)} %get-tuple-element.11.unit, ...), custom_call_target="tpu_custom_call" | custom-call | tf_op jit(solution)/shard_map/finish/pallas_call | solution.py:758

commit v9 on v8

--- a/solution.py
+++ b/solution.py
@@ -92,6 +92,12 @@
         remote(src, dst, send, recv, device).start()
 
 
+def unrolled(low, high, body, carry):
+    for n in range(low, high):
+        carry = body(n, carry)
+    return carry
+
+
 def greet(device):
     pl.semaphore_signal(pltpu.get_barrier_semaphore(), inc=1, device_id=device, device_id_type=MESH)
 
@@ -101,7 +107,7 @@
         greet(at.plane(n))
         return carry
 
-    lax.fori_loop(1, COLS, plane, 0)
+    unrolled(1, COLS, plane, 0)
 
     def worker(n, carry):
         core, zz = lax.div(n, 4), lax.rem(n, 4)
@@ -112,21 +118,18 @@
 
         return carry
 
-    lax.fori_loop(0, 8, worker, 0)
+    unrolled(0, 8, worker, 0)
 
     def home(n, carry):
         greet(at.home(n * 2 + 1 - at.e))
         return carry
 
-    lax.fori_loop(0, 4, home, 0)
+    unrolled(0, 4, home, 0)
 
     @pl.when(jnp.logical_not(at.stays))
     def _():
-        def column(n, carry):
+        for n in range(COLS):
             greet(at.swapped(n))
-            return carry
-
-        lax.fori_loop(0, COLS, column, 0)
 
     return jnp.where(at.stays, COLS - 1 + 7 + 4, COLS - 1 + 8 + 4 + COLS)
 
@@ -138,7 +141,7 @@
         send_or_copy(here, source.at[t], slot, send.at[t], recv.at[at.c], at.swapped(t))
         return carry
 
-    lax.fori_loop(0, COLS, column, 0)
+    unrolled(0, COLS, column, 0)
 
 
 def exchange_arrived(landing, recv):
@@ -146,7 +149,7 @@
         arrived(landing.at[n], recv.at[n])
         return carry
 
-    lax.fori_loop(0, COLS, column, 0)
+    unrolled(0, COLS, column, 0)
 
 
 def exchange_sent(at, source, send):
@@ -159,7 +162,7 @@
 
         return carry
 
-    lax.fori_loop(0, COLS, column, 0)
+    unrolled(0, COLS, column, 0)
 
 
 def repeat_heads(w_bias_t):
@@ -334,7 +337,7 @@
         )
         return carry
 
-    lax.fori_loop(0, 8, to_workers, 0)
+    unrolled(0, 8, to_workers, 0)
     lane = lax.broadcasted_iota(jnp.int32, (8, C), 1)
     packed_flags = jnp.where(
         lane == 0, m.flags[0:8, :], jnp.where(lane == 1, m.flags[8:16, :], m.flags[16:24, :])
@@ -569,7 +572,7 @@
         remote(piece(m.proj_b, t), m.r5.at[n], send.p1.at[n], recv.p1.at[n], at.plane(n)).start()
         return carry
 
-    lax.fori_loop(1, COLS, scatter_proj, 0)
+    unrolled(1, COLS, scatter_proj, 0)
     scatter_near(0)
     back(0)
     scatter_near(1)
@@ -578,14 +581,14 @@
         arrived(m.r5.at[n], recv.p1.at[n])
         return total + m.r5[n].astype(F32)
 
-    m.v5[...] = lax.fori_loop(1, COLS, proj_arrived, piece(m.proj, at.c)[...])
+    m.v5[...] = unrolled(1, COLS, proj_arrived, piece(m.proj, at.c)[...])
 
     def proj_to_homes(z, carry):
         slot = e * 4 + at.zz
         send_or_copy(at.is_home(z), m.v5, m.r6.at[slot], send.p2.at[z], recv.p2.at[slot], at.home(z))
         return carry
 
-    lax.fori_loop(0, ROWS, proj_to_homes, 0)
+    unrolled(0, ROWS, proj_to_homes, 0)
 
     back(1)
     halves = [plane_sum(0), plane_sum(1)]
@@ -605,14 +608,14 @@
         )
         return carry
 
-    lax.fori_loop(0, ROWS, to_homes, 0)
+    unrolled(0, ROWS, to_homes, 0)
 
 
     def share_arrived(n, total):
         arrived(m.r6.at[n], recv.p2.at[n])
         return total + m.r6[n]
 
-    m.v6[...] = lax.fori_loop(0, 8, share_arrived, jnp.zeros((16, 2 * HD), F32)).astype(BF16)
+    m.v6[...] = unrolled(0, 8, share_arrived, jnp.zeros((16, 2 * HD), F32)).astype(BF16)
     own_piece = piece(proj_out, at.c)
     pltpu.make_async_copy(m.v6, own_piece, recv.p3.at[0]).start()
 
@@ -620,7 +623,7 @@
         remote(m.v6, own_piece, send.p3.at[n], recv.p3.at[n], at.plane(n)).start()
         return carry
 
-    lax.fori_loop(1, COLS, spread, 0)
+    unrolled(1, COLS, spread, 0)
 
     for core in range(2):
         for zz in range(4):

time: 64.3 us -> 63.8 us (level); the launches traced: 64 us -> 62.8 us
  Pallas kernels: 62.7 us -> 61.5 us
    pallas_call x1, Pallas kernels: 58.9 us -> 57.7 us  [shards(): pl.pallas_call(main_kernel, out_shape=[landing, jax.ShapeDtypeStruct((C,...]
where the time goes in v9:
time: 63.8 us; the launch traced here: 62.8 us
  Pallas kernels  61.5 us (96%)
  between operations  1.29 us (2%)
    pallas_call x1, Pallas kernels, shards(): pl.pallas_call(main_kernel, out_shape=[landing, jax.ShapeDtypeStruct((C,...  57.7 us
    pallas_call x1, Pallas kernels, shards(): pl.pallas_call(finish_kernel, out_shape=[result, result, proj_shape], gri...  3.8 us

profile of v9, /device:TPU:1, one launch (start us, length us, event | category | flops | bytes accessed | tf_op | source)
XLA Modules:
  0.0 62.8 jit_solution(8328583079273658682)
XLA Ops:
  1.3 57.7 %main.1 = (bf16[16,3,48,128]{3,2,1,0:T(8,128)(2,1)}, bf16[128,512]{1,0:T(8,128)(2,1)}, f32[24,256]{1,0:T(8,128)}, f32[48,24,128]{2,1,0:T(8,128)}, f32[48,24,128]{2,1,0:T(8,128)}) custom-call(s32[1]{0:T(128)S(6)} %copy.13.refs_0_, bf16[48,24,128]{2,1,0:T(8,128)(2,1)} %refs_1_.1, bf16[48,24,128]{2,1,0:T(8,128)(2,1)} %refs_2_.1, s32[1,24]{1,0:T(1,128)} %bitcast.9, ...), custom_call_target="tpu_custom_call" | custom-call | tf_op jit(solution)/shard_map/main/pallas_call | solution.py:725
  59.0 3.8 %finish.1 = (bf16[48,24,128]{2,1,0:T(8,128)(2,1)}, bf16[48,24,128]{2,1,0:T(8,128)(2,1)}, f32[128,512]{1,0:T(8,128)}) custom-call(bf16[16,3,48,128]{3,2,1,0:T(8,128)(2,1)} %get-tuple-element.8.land, bf16[128,512]{1,0:T(8,128)(2,1)} %get-tuple-element.9.proj_in, f32[24,256]{1,0:T(8,128)} %get-tuple-element.10.h_sum, f32[48,24,128]{2,1,0:T(8,128)} %get-tuple-element.11.unit, ...), custom_call_target="tpu_custom_call" | custom-call | tf_op jit(solution)/shard_map/finish/pallas_call | solution.py:761

commit v10 on v9

--- a/solution.py
+++ b/solution.py
@@ -192,14 +192,13 @@
 
 
 MAIN_SCRATCH = dict(
-    pair=((TALL, WIDTH, C), BF16),
-    cot=((TALL, WIDTH, C), BF16),
+    pair=((TALL * WIDTH, C), BF16),
+    cot=((TALL * WIDTH, C), BF16),
     residues=((1, WIDTH), jnp.int32),
     gain=((1, C), F32),
     shift=((1, C), F32),
     w_proj=((C, 4 * HD), BF16),
     gate_bias=((1, HD), F32),
-    w_bias_t=((H, C), BF16),
     w_out=((HD, C), BF16),
     home_unit=((TALL, WIDTH, C), F32),
     home_rstd=((TALL, WIDTH, C), F32),
@@ -254,7 +253,7 @@
     out=((COLS, OWN, 2 * WIDTH, C), BF16),
 )
 MAIN_SEMS = dict(
-    operand=(9,),
+    operand=(8,),
     norm=(2,),
     in1=(COLS,),
     in2=(COLS,),
@@ -280,7 +279,7 @@
 
 
 def main_kernel(*refs):
-    length, operands = refs[0], refs[1:MAIN_IN]
+    length, w_bias_t, operands = refs[0], refs[1], refs[2:MAIN_IN]
     (land, proj_out, h_sum, unit_out, rstd_out) = refs[MAIN_IN : MAIN_IN + MAIN_OUT]
     rest = refs[MAIN_IN + MAIN_OUT :]
     m, send, recv = Names(), Names(), Names()
@@ -291,15 +290,16 @@
         setattr(send, name, ref)
     for name, ref in zip(MAIN_SEMS, rest[len(MAIN_SEMS) :]):
         setattr(recv, name, ref)
-    held = (m.pair, m.cot, m.residues, m.gain, m.shift, m.w_proj, m.gate_bias, m.w_bias_t, m.w_out)
-    pair, cot, residues, gain, shift, w_proj, gate_bias, w_bias_t, w_out = held
-    for n in range(MAIN_IN - 1):
-        pltpu.make_async_copy(operands[n], held[n], recv.operand.at[n]).start()
+    held = (m.pair, m.cot, m.residues, m.gain, m.shift, m.w_proj, m.gate_bias, m.w_out)
+    pair, cot, residues, gain, shift, w_proj, gate_bias, w_out = held
+    loads = [pltpu.make_async_copy(operands[n], held[n], recv.operand.at[n]) for n in range(len(held))]
+    for load in loads:
+        load.start()
     at = Place()
     e = at.e
     count = greet_all(at)
-    for n in range(MAIN_IN - 1):
-        arrived(held[n], recv.operand.at[n])
+    for load in loads:
+        load.wait()
 
     sublane = lax.broadcasted_iota(jnp.int32, (WIDTH, WIDTH), 0)
     lane = lax.broadcasted_iota(jnp.int32, (WIDTH, WIDTH), 1)
@@ -731,7 +731,7 @@
             block,
             block,
         ],
-        in_specs=[pl.BlockSpec(memory_space=pltpu.SMEM)] + [any_space] * (MAIN_IN - 1),
+        in_specs=[pl.BlockSpec(memory_space=pltpu.SMEM)] + vmem(1) + [any_space] * (MAIN_IN - 2),
         out_specs=[any_space] * 2 + vmem(1) + [any_space] * 2,
         scratch_shapes=[pltpu.VMEM(shape, dtype) for shape, dtype in MAIN_SCRATCH.values()] + sems + sems,
         compiler_params=pltpu.CompilerParams(
@@ -740,14 +740,14 @@
         name="main",
     )(
         valid_length,
-        pair_act,
-        cotangent,
+        w_bias.T,
+        pair_act.reshape(TALL * WIDTH, C),
+        cotangent.reshape(TALL * WIDTH, C),
         residue_mask.reshape(1, WIDTH),
         gain,
         ln_shift.reshape(1, C),
         w_proj,
         gate_bias.reshape(1, HD),
-        w_bias.T,
         w_out,
     )
     result = jax.ShapeDtypeStruct(pair_act.shape, BF16)

time: 63.8 us -> 64.4 us (level)
  Pallas kernels: 61.5 us -> 62.2 us
    pallas_call x1, Pallas kernels: 57.7 us -> 58.4 us  [shards(): pl.pallas_call(main_kernel, out_shape=[landing, jax.ShapeDtypeStruct((C,...]
where the time goes in v10:
time: 64.4 us; the launch traced here: 63.5 us
  Pallas kernels  62.2 us (97%)
  between operations  1.29 us (2%)
    pallas_call x1, Pallas kernels, shards(): pl.pallas_call(main_kernel, out_shape=[landing, jax.ShapeDtypeStruct((C,...  58.4 us
    pallas_call x1, Pallas kernels, shards(): pl.pallas_call(finish_kernel, out_shape=[result, result, proj_shape], gri...  3.81 us

profile of v10, /device:TPU:1, one launch (start us, length us, event | category | flops | bytes accessed | tf_op | source)
XLA Modules:
  0.0 63.5 jit_solution(6473560077776345037)
XLA Ops:
  1.3 58.4 %main.1 = (bf16[16,3,48,128]{3,2,1,0:T(8,128)(2,1)}, bf16[128,512]{1,0:T(8,128)(2,1)}, f32[24,256]{1,0:T(8,128)}, f32[48,24,128]{2,1,0:T(8,128)}, f32[48,24,128]{2,1,0:T(8,128)}) custom-call(s32[1]{0:T(128)S(6)} %copy.13.refs_0_, bf16[4,128]{1,0:T(4,128)(2,1)} %bitcast.9, bf16[1152,128]{1,0:T(8,128)(2,1)} %bitcast.7, bf16[1152,128]{1,0:T(8,128)(2,1)} %bitcast.8, ...), custom_call_target="tpu_custom_call" | custom-call | tf_op jit(solution)/shard_map/main/pallas_call | solution.py:725
  59.6 3.8 %finish.1 = (bf16[48,24,128]{2,1,0:T(8,128)(2,1)}, bf16[48,24,128]{2,1,0:T(8,128)(2,1)}, f32[128,512]{1,0:T(8,128)}) custom-call(bf16[16,3,48,128]{3,2,1,0:T(8,128)(2,1)} %get-tuple-element.8.land, bf16[128,512]{1,0:T(8,128)(2,1)} %get-tuple-element.9.proj_in, f32[24,256]{1,0:T(8,128)} %get-tuple-element.10.h_sum, f32[48,24,128]{2,1,0:T(8,128)} %get-tuple-element.11.unit, ...), custom_call_target="tpu_custom_call" | custom-call | tf_op jit(solution)/shard_map/finish/pallas_call | solution.py:761
